TPU v7x, 32 devices: a whole 2x2x4 slice. The times are simulated.
32 devices in a mesh: chip: 16 (over z, y, x), cores: 2 (over core).
Axes of the slice: x: 2, y: 2, z: 4, core: 2. Of those that a mesh axis runs over, the one named last changes fastest.
Arguments:
- patch_field: float32 [512, 6, 128, 128], P(('chip', 'cores')), may hold values from -6 to 6
- patch_tables: float32 [512, 6, 128, 128], P(('chip', 'cores')), may hold values from -0.5 to 0.5
- coupling: float32 [512, 5, 6, 6], P(('chip', 'cores')), may hold values from -1 to 1
- side_device: int32 [4096, 1], replicated, may hold values from 0 to 31; in each aligned block of 128 rows (0 to 127, 128 to 255, ...) at most 8 rows name the same one
- side_detail: int32 [4096, 4], replicated, may hold values from 0 to 96, as said below
- penalty: float32 [2048, 2, 128], P(('chip', 'cores')), may hold values from 0.1 to 1
- angles: float32 [2048, 3], P(('chip', 'cores')), may hold values from -3.140625 to 3.140625
Outputs:
- response: float32 [512, 6, 128, 128], P(('chip', 'cores'))
Inputs may be any that keep to these rules, and one draw needn't show every extreme that they name: `side_device`: in each aligned block of 128 rows (the sides of the interfaces whose quadrature one device owns) no device is named by more than 8 rows, and some device is named by exactly 8 rows. Each owner has exactly 128 sides. `side_detail`: column 0 is below 16, column 1 below 4, column 2 below 32, column 3 from 64 to 96.
All inputs are finite; a program needn't handle non-finite values.
Results may differ from a plain program's by a relative error of at most 0.0003.
Values sent between devices are 32-bit elements; how exact they have to be, the bound alone decides.
No kernel may reach another device: no remote copies, remote signals or barrier semaphores. Data moves between devices by JAX's collectives and lax.ppermute only.
A program may use at most 192 MiB of HBM per device.

v0:
```python
import functools

import jax
import jax.numpy as jnp
from jax import lax
from jax.experimental import pallas as pl
from jax.experimental.pallas import tpu as pltpu
from jax.sharding import PartitionSpec as P

F32 = jnp.float32
BF16 = jnp.bfloat16
I32 = jnp.int32
EDGES = 4
LANES = 128
ROWS = 8
VMEM_LIMIT = 48 * 1024 * 1024


def iota(shape, axis):
    return lax.broadcasted_iota(I32, shape, axis)


def halves(values):
    high = values.astype(BF16)
    low = (values - high.astype(F32)).astype(BF16)
    return high, low


def dot(left, right):
    return lax.dot_general(left, right, (((1,), (0,)), ((), ())), preferred_element_type=F32)


def dot_nt(left, right):
    return lax.dot_general(left, right, (((1,), (1,)), ((), ())), preferred_element_type=F32)


def lane_gather(values, index):
    return jnp.take_along_axis(values, index, axis=1)


class Codes:
    def __init__(self, per_device, points):
        self.bits = (points - 1).bit_length()
        self.local_bits = max(1, (per_device - 1).bit_length())
        self.mask = (1 << self.bits) - 1
        self.at_start = self.bits
        self.at_edge = 2 * self.bits
        self.at_local = self.at_edge + 2
        self.at_device = self.at_local + self.local_bits

    def pack(self, device, detail):
        return (
            (device << self.at_device)
            | (detail[..., 0] << self.at_local)
            | (detail[..., 1] << self.at_edge)
            | (detail[..., 2] << self.at_start)
            | detail[..., 3]
        )

    def length(self, code):
        return code & self.mask

    def start(self, code):
        return (code >> self.at_start) & self.mask

    def edge(self, code):
        return (code >> self.at_edge) & 3

    def local(self, code):
        return (code >> self.at_local) & ((1 << self.local_bits) - 1)

    def device(self, code):
        return code >> self.at_device


def slot_tables(fields, code, me, capacity, per_device):
    owners, _, sides = code.shape
    slots = owners * capacity
    spread = jnp.broadcast_to(code, (owners, capacity, sides)).reshape(slots, sides)
    mine = fields.device(spread) == me
    earlier = (iota((sides, sides), 0) < iota((sides, sides), 1)).astype(F32).astype(BF16)
    rank = dot(mine.astype(F32).astype(BF16), earlier).astype(I32)
    wanted = iota((slots, sides), 0) % capacity
    row = fields.edge(spread) * per_device + fields.local(spread) + 1
    value = (fields.start(spread) << 16) | row
    chosen = jnp.where(mine & (rank == wanted), value.astype(F32), 0.0)
    found = jnp.sum(chosen, axis=1, keepdims=True).astype(I32)
    return (found & 0xFFFF) - 1, found >> 16


def fold_window(tiles, last_pieces, window):
    lane = iota(tiles[0].shape, 1)
    out = []
    for at in range(5):
        if at < 4:
            out.append(jnp.where(lane < window, tiles[at], last_pieces[at]))
        else:
            out.append(tiles[at])
    return out


def unfold_last(tiles, window):
    quarter = window // 4
    lane = iota(tiles[0].shape, 1)
    lanes = tiles[0].shape[1]
    value = None
    for at in range(4):
        shift = (lanes - (window - quarter * at)) % lanes
        piece = pltpu.roll(tiles[at], shift, 1)
        value = piece if value is None else jnp.where(lane >= quarter * at, piece, value)
    return value


def pack_kernel(cfg, me_ref, code_ref, field_ref, out_ref, strips_ref):
    fields, per_device, capacity, window, batch, points = cfg
    step = pl.program_id(0)
    lane = iota((16, points), 1)
    sub = iota((16, points), 0)
    first = jnp.where(lane == 0, 1.5, jnp.where(lane == 1, -0.5, 0.0))
    second = jnp.where(lane == points - 1, 1.5, jnp.where(lane == points - 2, -0.5, 0.0))
    select = jnp.where(sub == 0, first, jnp.where(sub == 1, second, 0.0)).astype(BF16)
    select = jnp.concatenate([select, select], axis=1)
    for b in range(batch):
        patch = step * batch + b
        block = field_ref[b].reshape(6 * points, points)
        high, low = halves(block)
        columns = dot_nt(select, jnp.concatenate([high, low], axis=1))
        top = [1.5 * field_ref[b, c, 0:1, :] - 0.5 * field_ref[b, c, 1:2, :] for c in range(6)]
        bottom = [
            1.5 * field_ref[b, c, points - 1 : points, :]
            - 0.5 * field_ref[b, c, points - 2 : points - 1, :]
            for c in range(6)
        ]
        for c in range(6):
            cols = slice(c * points, (c + 1) * points)
            strips_ref[c, pl.ds(patch, 1), :] = top[c]
            strips_ref[c, pl.ds(per_device + patch, 1), :] = bottom[c]
            strips_ref[c, pl.ds(2 * per_device + patch, 1), :] = columns[0:1, cols]
            strips_ref[c, pl.ds(3 * per_device + patch, 1), :] = columns[1:2, cols]

    @pl.when(step == pl.num_programs(0) - 1)
    def _():
        edges = EDGES * per_device
        row, start = slot_tables(fields, code_ref[...], me_ref[0], capacity, per_device)
        slots = row.shape[0]
        owners = slots // capacity
        picker = jnp.where(iota((slots, 2 * edges), 1) % edges == row, 1.0, 0.0).astype(BF16)
        high, low = halves(jnp.concatenate([strips_ref[c] for c in range(6)], axis=1))
        picked = dot(picker, jnp.concatenate([high, low], axis=0))
        base = iota((slots, points), 1) + start - 1
        quarter = window // 4
        tiles = [
            lane_gather(picked[:, c * points : (c + 1) * points], base & (points - 1))
            for c in range(5)
        ]
        last = picked[:, 5 * points :]
        pieces = [
            lane_gather(last, (base - (window - quarter * at)) & (points - 1)) for at in range(4)
        ]
        for at, tile in enumerate(fold_window(tiles, pieces, window)):
            out_ref[:, at * capacity : (at + 1) * capacity, :] = tile.reshape(
                owners, capacity, points
            )


def read_slots(ref, capacity, window):
    owners, rows, lanes = ref.shape
    tiles = [
        ref[:, at * capacity : (at + 1) * capacity, :].reshape(owners * capacity, lanes)
        for at in range(5)
    ]
    tiles.append(unfold_last(tiles, window))
    return tiles


def spline_weight(offset):
    magnitude = jnp.abs(offset)
    inner = 0.75 - magnitude * magnitude
    outer = 0.5 * jnp.square(jnp.maximum(1.5 - magnitude, 0.0))
    return jnp.where(magnitude < 0.5, inner, outer)


def owner_kernel(cfg, me_ref, code_ref, arrived_ref, penalty_ref, frame_ref, out_ref, work_ref):
    fields, per_device, capacity, window, points = cfg
    sides = code_ref.shape[2]
    owned = sides // 2
    owners = arrived_ref.shape[0]
    slots = owners * capacity
    code_row = jnp.broadcast_to(code_ref[me_ref[0]], (sides, sides))
    code = jnp.transpose(code_row)
    device, device_row = fields.device(code), fields.device(code_row)
    same = device == device_row
    sub, lane = iota((sides, sides), 0), iota((sides, sides), 1)
    rank = jnp.sum(jnp.where(same & (lane < sub), 1.0, 0.0), axis=1, keepdims=True).astype(I32)
    rank_row = jnp.sum(jnp.where(same & (sub < lane), 1.0, 0.0), axis=0, keepdims=True).astype(I32)
    slot = device[:, 0:1] * capacity + rank
    slot_row = device_row[0:1] * capacity + rank_row
    taker = jnp.where(iota((sides, 2 * slots), 1) % slots == slot, 1.0, 0.0).astype(BF16)
    giver = jnp.where(iota((slots, sides), 0) == slot_row, 1.0, 0.0).astype(BF16)

    tiles = jnp.concatenate(read_slots(arrived_ref, capacity, window), axis=1)
    high, low = halves(tiles)
    taken = dot(taker, jnp.concatenate([high, low], axis=0))

    start = fields.start(code)
    length = fields.length(code).astype(F32)
    quad = iota((sides, points), 1)
    param = (quad.astype(F32) + 0.5) * length * (1.0 / points)
    centre = (param + 0.5).astype(I32)
    offset = param - centre.astype(F32)
    before = jnp.where(start + centre >= 1, 0.5 * jnp.square(0.5 - offset), 0.0)
    middle = 0.75 - offset * offset
    after = jnp.where(start + centre + 1 < points, 0.5 * jnp.square(0.5 + offset), 0.0)
    for c in range(6):
        values = taken[:, c * points : (c + 1) * points]
        work_ref[c] = (
            before * lane_gather(values, centre)
            + middle * lane_gather(values, centre + 1)
            + after * lane_gather(values, (centre + 2) & (points - 1))
        )

    frame = [jnp.broadcast_to(frame_ref[:, e : e + 1], (owned, points)) for e in range(9)]
    for b in range(2):
        ahead = [work_ref[3 * b + c, pl.ds(0, owned, stride=2), :] for c in range(3)]
        behind = [work_ref[3 * b + c, pl.ds(1, owned, stride=2), :] for c in range(3)]
        weight = penalty_ref[b]
        loads = [
            weight
            * (
                ahead[c]
                - (
                    frame[3 * c] * behind[0]
                    + frame[3 * c + 1] * behind[1]
                    + frame[3 * c + 2] * behind[2]
                )
            )
            for c in range(3)
        ]
        for c in range(3):
            work_ref[3 * b + c, pl.ds(0, owned, stride=2), :] = loads[c]
            work_ref[3 * b + c, pl.ds(1, owned, stride=2), :] = -(
                frame[c] * loads[0] + frame[3 + c] * loads[1] + frame[6 + c] * loads[2]
            )

    point = iota((sides, points), 1)
    centre_at = (point - 1).astype(F32)
    opening = jnp.floor((centre_at - 1.5) * (float(points) / length) - 0.5).astype(I32) + 1
    place = start + point - 1
    inside = (place >= 0) & (place < points)
    forces = [jnp.zeros((sides, points), F32) for _ in range(6)]
    for m in range(6):
        at = opening + m
        weight = spline_weight((at.astype(F32) + 0.5) * length * (1.0 / points) - centre_at)
        weight = jnp.where(inside & (at >= 0) & (at < points), weight, 0.0)
        index = at & (points - 1)
        for c in range(6):
            forces[c] = forces[c] + weight * lane_gather(work_ref[c], index)
    high, low = halves(jnp.concatenate(forces, axis=1))
    given = dot(jnp.concatenate([giver, giver], axis=1), jnp.concatenate([high, low], axis=0))
    tiles = [given[:, c * points : (c + 1) * points] for c in range(5)]
    last = given[:, 5 * points :]
    quarter = window // 4
    pieces = [pltpu.roll(last, window - quarter * at, 1) for at in range(4)]
    for at, tile in enumerate(fold_window(tiles, pieces, window)):
        out_ref[:, at * capacity : (at + 1) * capacity, :] = tile.reshape(owners, capacity, points)


def interior_kernel(cfg, coupling_ref, field_ref, table_ref, *rest):
    first, points = cfg
    out_ref, applied_ref, mixed_ref = rest[-3:]
    patch = pl.program_id(0) + first
    left = table_ref[0, 0:3].reshape(3 * points, points)
    left_high, left_low = halves(left)
    field_high, field_low = [], []
    for c in range(6):
        high, low = halves(field_ref[0, c])
        field_high.append(high)
        field_low.append(low)
    field_high = jnp.concatenate(field_high, axis=1)
    field_low = jnp.concatenate(field_low, axis=1)
    applied_ref[...] = dot(
        jnp.concatenate([left_high, left_low], axis=1),
        jnp.concatenate([field_high, field_high], axis=0),
    ) + dot(left_high, field_low)

    def weight(t, c, d):
        return coupling_ref[patch, (t * 6 + c) * 6 + d]

    chunk = 16
    for at in range(points // chunk):
        sums = [[None] * 6 for _ in range(3)]

        def add(group, c, value):
            have = sums[group][c]
            sums[group][c] = value if have is None else have + value

        for d in range(6):
            stiff, mass, slope = [
                applied_ref[
                    g * points + at * chunk : g * points + (at + 1) * chunk,
                    d * points : (d + 1) * points,
                ]
                for g in range(3)
            ]
            for c in range(6):
                add(0, c, weight(0, c, d) * stiff)
                add(0, c, weight(3, c, d) * mass)
                add(0, c, weight(4, c, d) * slope)
                add(1, c, weight(1, c, d) * mass)
                add(2, c, weight(2, c, d) * slope)
        for c in range(6):
            rows = pl.ds(c * points + at * chunk, chunk)
            for g in range(3):
                high, low = halves(sums[g][c])
                mixed_ref[rows, g * points : (g + 1) * points] = high
                mixed_ref[rows, (3 + g) * points : (4 + g) * points] = low

    right = jnp.concatenate([table_ref[0, 4], table_ref[0, 3], table_ref[0, 5]], axis=1)
    right_high, right_low = halves(right)
    right = jnp.concatenate([right_high, right_low], axis=0)
    both = dot_nt(mixed_ref[...], jnp.concatenate([right, right], axis=1))
    total = both[:, :points] + both[:, points:]
    out_ref[0] = total.reshape(6, points, points)


def finish_kernel(cfg, me_ref, code_ref, arrived_ref, inner_ref, out_ref, edge_ref, turned_ref):
    fields, per_device, capacity, window, batch, points = cfg
    step = pl.program_id(0)
    edges = EDGES * per_device

    @pl.when(step == 0)
    def _():
        row, start = slot_tables(fields, code_ref[...], me_ref[0], capacity, per_device)
        slots = row.shape[0]
        picker = jnp.where(iota((slots, 2 * edges), 1) % edges == row, 1.0, 0.0)
        picker = jnp.transpose(picker)[:edges].astype(BF16)
        at = iota((slots, points), 1) - start + 1
        valid = (at >= 0) & (at < window)
        index = at & (points - 1)
        tiles = [
            jnp.where(valid, lane_gather(tile, index), 0.0)
            for tile in read_slots(arrived_ref, capacity, window)
        ]
        high, low = halves(jnp.concatenate(tiles, axis=1))
        total = dot(
            jnp.concatenate([picker, picker], axis=1), jnp.concatenate([high, low], axis=0)
        )
        for c in range(6):
            edge_ref[c] = total[:, c * points : (c + 1) * points]
            part = total[2 * per_device :, c * points : (c + 1) * points]
            high = part.astype(BF16).astype(F32)
            both = jnp.concatenate([high, part - high], axis=0)
            turned_ref[c] = jnp.transpose(both).astype(BF16)

    width = batch * points
    kk = iota((edges, width), 0)
    at = iota((edges, width), 1)
    lane = at % points
    hit = (kk % per_device) == (step * batch + at // points)
    low_edge = (kk // per_device) % 2 == 0
    near = lane == jnp.where(low_edge, 0, points - 1)
    next_to = lane == jnp.where(low_edge, 1, points - 2)
    select = jnp.where(hit & near, 1.5, jnp.where(hit & next_to, -0.5, 0.0)).astype(BF16)
    sub = iota((ROWS, points), 0)
    for c in range(6):
        add = dot(turned_ref[c], select)
        for b in range(batch):
            patch = step * batch + b
            value = inner_ref[b, c] + add[:, b * points : (b + 1) * points]
            out_ref[b, c] = value
            top = jnp.broadcast_to(edge_ref[c, pl.ds(patch, 1), :], (ROWS, points))
            bottom = jnp.broadcast_to(edge_ref[c, pl.ds(per_device + patch, 1), :], (ROWS, points))
            out_ref[b, c, 0:ROWS] = value[0:ROWS] + jnp.where(
                sub == 0, 1.5 * top, jnp.where(sub == 1, -0.5 * top, 0.0)
            )
            out_ref[b, c, points - ROWS :] = value[points - ROWS :] + jnp.where(
                sub == ROWS - 1, 1.5 * bottom, jnp.where(sub == ROWS - 2, -0.5 * bottom, 0.0)
            )


def frames(angle_data):
    cos_a, sin_a = jnp.cos(angle_data[:, 0]), jnp.sin(angle_data[:, 0])
    cos_b, sin_b = jnp.cos(angle_data[:, 1]), jnp.sin(angle_data[:, 1])
    cos_g, sin_g = jnp.cos(angle_data[:, 2]), jnp.sin(angle_data[:, 2])
    return jnp.stack(
        [
            cos_g * cos_b,
            cos_g * sin_b * sin_a - sin_g * cos_a,
            cos_g * sin_b * cos_a + sin_g * sin_a,
            sin_g * cos_b,
            sin_g * sin_b * sin_a + cos_g * cos_a,
            sin_g * sin_b * cos_a - cos_g * sin_a,
            -sin_b,
            cos_b * sin_a,
            cos_b * cos_a,
        ],
        axis=1,
    )


def exchange(payload):
    return lax.all_to_all(payload, ("chip", "cores"), split_axis=0, concat_axis=0, tiled=True)


def whole(shape):
    return pl.BlockSpec(shape, lambda *_: (0,) * len(shape))


def params():
    return pltpu.CompilerParams(vmem_limit_bytes=VMEM_LIMIT)


def shards(patch_field, patch_tables, coupling, side_device, side_detail, penalty, angles):
    devices = lax.axis_size(("chip", "cores"))
    me = lax.axis_index(("chip", "cores")).astype(I32).reshape(1)
    per_device, _, points, _ = patch_field.shape
    owned = penalty.shape[0]
    sides = 2 * owned
    capacity = -(-max(2, 2 * sides // devices) // ROWS) * ROWS
    window = 3 * points // 4 + 4
    fields = Codes(per_device, points)
    smem = pl.BlockSpec(memory_space=pltpu.SMEM)
    code = fields.pack(side_device[:, 0], side_detail).reshape(devices, 1, sides)
    payload_shape = (devices, 5 * capacity, points)
    payload = jax.ShapeDtypeStruct(payload_shape, F32)
    whole_field = jax.ShapeDtypeStruct(patch_field.shape, F32)
    coupling = coupling.reshape(per_device, -1)
    frame = frames(angles)
    weights = jnp.swapaxes(penalty, 0, 1)

    batch = 4
    outgoing = pl.pallas_call(
        functools.partial(pack_kernel, (fields, per_device, capacity, window, batch, points)),
        name="pack",
        out_shape=payload,
        grid=(per_device // batch,),
        in_specs=[
            smem,
            whole(code.shape),
            pl.BlockSpec((batch, 6, points, points), lambda i: (i, 0, 0, 0)),
        ],
        out_specs=whole(payload_shape),
        scratch_shapes=[pltpu.VMEM((6, EDGES * per_device, points), F32)],
        compiler_params=params(),
    )(me, code, patch_field)

    def interior(begin, end, into, after):
        count = end - begin
        tied = lax.optimization_barrier((coupling, after))[0]
        block = pl.BlockSpec((1, 6, points, points), lambda i: (i + begin, 0, 0, 0))
        given = [] if into is None else [into]
        return pl.pallas_call(
            functools.partial(interior_kernel, (begin, points)),
            name="interior",
            out_shape=whole_field,
            grid=(count,),
            in_specs=[smem, block, block] + [pl.BlockSpec(memory_space=pl.ANY)] * len(given),
            out_specs=block,
            scratch_shapes=[
                pltpu.VMEM((3 * points, 6 * points), F32),
                pltpu.VMEM((6 * points, 6 * points), BF16),
            ],
            input_output_aliases={3: 0} if given else {},
            compiler_params=params(),
            cost_estimate=pl.CostEstimate(
                flops=count * 6 * 6 * 6 * points**3,
                bytes_accessed=count * 18 * points * points * 4,
                transcendentals=0,
            ),
        )(tied, patch_field, patch_tables, *given)

    half = per_device // 2
    arrived = exchange(outgoing)
    inner = interior(0, half, None, outgoing)
    weights, inner = lax.optimization_barrier((weights, inner))
    back = pl.pallas_call(
        functools.partial(owner_kernel, (fields, per_device, capacity, window, points)),
        name="owner",
        out_shape=payload,
        in_specs=[smem] + [pl.BlockSpec(memory_space=pltpu.VMEM)] * 4,
        out_specs=pl.BlockSpec(memory_space=pltpu.VMEM),
        scratch_shapes=[pltpu.VMEM((6, sides, points), F32)],
        compiler_params=params(),
    )(me, code, arrived, weights, frame)
    returned = exchange(back)
    inner = interior(half, per_device, inner, back)
    batch = 4
    block = pl.BlockSpec((batch, 6, points, points), lambda i: (i, 0, 0, 0))
    return pl.pallas_call(
        functools.partial(finish_kernel, (fields, per_device, capacity, window, batch, points)),
        name="finish",
        out_shape=whole_field,
        grid=(per_device // batch,),
        in_specs=[smem, whole(code.shape), whole(payload_shape), block],
        out_specs=block,
        scratch_shapes=[
            pltpu.VMEM((6, EDGES * per_device, points), F32),
            pltpu.VMEM((6, points, EDGES * per_device), BF16),
        ],
        input_output_aliases={3: 0},
        compiler_params=params(),
    )(me, code, returned, inner)


def solution(mesh):
    return jax.shard_map(
        shards,
        mesh=mesh,
        in_specs=(
            P(("chip", "cores"), None, None, None),
            P(("chip", "cores"), None, None, None),
            P(("chip", "cores"), None, None, None),
            P(),
            P(),
            P(("chip", "cores"), None, None),
            P(("chip", "cores"), None),
        ),
        out_specs=P(("chip", "cores"), None, None, None),
        check_vma=False,
    )
```

profile of v0, /device:TPU:0, one launch (start us, length us, event | category | flops | bytes accessed | tf_op | source)
XLA Modules:
  0.0 77.6 jit_solution(12508069743469740824)
XLA Ops:
  0.0 0.0 copy-start.2
  0.0 0.0 copy-start.1
  0.0 0.0 copy-start
  0.0 1.1 %or_bitcast_fusion.code_ref = s32[32,1,128]{2,1,0:T(1,128)S(1)} fusion(s32[4096,4]{0,1:T(4,128)} %param.11, s32[4096,1]{0,1:T(1,128)} %param.10), kind=kLoop, calls=%fused_computation.1 | loop fusion | flops 32768 | bytes 98304 | tf_op jit(solution)/shard_map/or | solution.py:53
  1.1 6.7 %pack.1 = f32[32,40,128]{2,1,0:T(8,128)} custom-call(s32[1]{0:T(128)} %bitcast.me_ref, s32[32,1,128]{2,1,0:T(1,128)S(1)} %or_bitcast_fusion.code_ref, f32[16,6,128,128]{3,2,1,0:T(8,128)} %field_ref.5), custom_call_target="tpu_custom_call" | custom-call | tf_op jit(solution)/shard_map/pack/pallas_call | solution.py:432
  7.7 7.3 %all-to-all-start = ((f32[32,40,128]{2,1,0:T(8,128)}), f32[32,40,128]{2,1,0:T(8,128)S(1)}, u32[]{:S(2)}, u32[]{:S(2)}) async-start(f32[32,40,128]{2,1,0:T(8,128)} %pack.1), calls=%async_computation | async-start | bytes 1310720 | tf_op jit(solution)/shard_map/all_to_all | solution.py:402
  15.0 0.0 copy-done.2
  15.0 0.1 fusion.3
  15.1 0.1 fusion
  15.2 0.1 copy.23.frame_ref
  15.3 0.0 copy-done.1
  15.3 0.0 copy-done
  15.4 0.1 copy.22.coupling_ref
  15.4 22.2 %interior.2.rest_0_ = f32[16,6,128,128]{3,2,1,0:T(8,128)} custom-call(f32[16,180]{1,0:T(8,128)S(1)} %copy.22.coupling_ref, f32[16,6,128,128]{3,2,1,0:T(8,128)} %field_ref.5, f32[16,6,128,128]{3,2,1,0:T(8,128)} %table_ref.3), custom_call_target="tpu_custom_call" | custom-call | flops 3623878656 | bytes 9437184 | tf_op jit(solution)/shard_map/interior/pallas_call | solution.py:452
  37.6 0.0 all-to-all-done.arrived_ref
  37.6 4.3 %owner.1 = f32[32,40,128]{2,1,0:T(8,128)} custom-call(s32[1]{0:T(128)} %bitcast.me_ref, s32[32,1,128]{2,1,0:T(1,128)S(1)} %or_bitcast_fusion.code_ref, f32[32,40,128]{2,1,0:T(8,128)S(1)} %all-to-all-done.arrived_ref, f32[2,64,128]{2,1,0:T(8,128)S(1)} %bitcast.8, f32[64,9]{1,0:T(8,128)S(1)} %copy.23.frame_ref), custom_call_target="tpu_custom_call" | custom-call | tf_op jit(solution)/shard_map/owner/pallas_call | solution.py:476
  41.9 5.8 %all-to-all-start.1 = ((f32[32,40,128]{2,1,0:T(8,128)}), f32[32,40,128]{2,1,0:T(8,128)S(1)}, u32[]{:S(2)}, u32[]{:S(2)}) async-start(f32[32,40,128]{2,1,0:T(8,128)} %owner.1), calls=%async_computation.1 | async-start | bytes 1310720 | tf_op jit(solution)/shard_map/all_to_all | solution.py:402
  47.8 0.1 copy.24.coupling_ref
  47.8 22.2 %interior.3.inner_ref = f32[16,6,128,128]{3,2,1,0:T(8,128)} custom-call(f32[16,180]{1,0:T(8,128)S(1)} %copy.24.coupling_ref, f32[16,6,128,128]{3,2,1,0:T(8,128)} %field_ref.5, f32[16,6,128,128]{3,2,1,0:T(8,128)} %table_ref.3, f32[16,6,128,128]{3,2,1,0:T(8,128)} %interior.2.rest_0_), custom_call_target="tpu_custom_call", output_to_operand_aliasing={{}: (3, {})} | custom-call | flops 3623878656 | bytes 9437184 | tf_op jit(solution)/shard_map/interior/pallas_call | solution.py:452
  70.0 0.0 all-to-all-done.1.arrived_ref
  70.0 7.5 %finish.1 = f32[16,6,128,128]{3,2,1,0:T(8,128)} custom-call(s32[1]{0:T(128)} %bitcast.me_ref, s32[32,1,128]{2,1,0:T(1,128)S(1)} %or_bitcast_fusion.code_ref, f32[32,40,128]{2,1,0:T(8,128)S(1)} %all-to-all-done.1.arrived_ref, f32[16,6,128,128]{3,2,1,0:T(8,128)} %interior.3.inner_ref), custom_call_target="tpu_custom_call", output_to_operand_aliasing={{}: (3, {})} | custom-call | tf_op jit(solution)/shard_map/finish/pallas_call | solution.py:489
  (3 shorter events, 0.1 us)
Async XLA Ops:
  0.0 15.0 %copy-start.2 = (f32[64,3]{0,1:T(4,128)S(1)}, f32[64,3]{0,1:T(4,128)}, u32[]{:S(2)}) copy-start(f32[64,3]{0,1:T(4,128)} %param.13) | copy-start | bytes 2308
  0.0 15.3 %copy-start.1 = (f32[64,2,128]{2,1,0:T(2,128)S(1)}, f32[64,2,128]{2,1,0:T(2,128)}, u32[]{:S(2)}) copy-start(f32[64,2,128]{2,1,0:T(2,128)} %param.12) | copy-start | bytes 196612
  0.0 15.3 %copy-start = (f32[16,5,6,6]{0,3,2,1:T(8,128)S(1)}, f32[16,5,6,6]{0,3,2,1:T(8,128)}, u32[]{:S(2)}) copy-start(f32[16,5,6,6]{0,3,2,1:T(8,128)} %param.9) | copy-start | bytes 34564
  7.7 29.9 %all-to-all-start = ((f32[32,40,128]{2,1,0:T(8,128)}), f32[32,40,128]{2,1,0:T(8,128)S(1)}, u32[]{:S(2)}, u32[]{:S(2)}) async-start(f32[32,40,128]{2,1,0:T(8,128)} %pack.1), calls=%async_computation | async-start | bytes 1310720 | tf_op jit(solution)/shard_map/all_to_all | solution.py:402
  41.9 28.1 %all-to-all-start.1 = ((f32[32,40,128]{2,1,0:T(8,128)}), f32[32,40,128]{2,1,0:T(8,128)S(1)}, u32[]{:S(2)}, u32[]{:S(2)}) async-start(f32[32,40,128]{2,1,0:T(8,128)} %owner.1), calls=%async_computation.1 | async-start | bytes 1310720 | tf_op jit(solution)/shard_map/all_to_all | solution.py:402
where the time goes:
time: 77.9 us; the launch traced here: 77.6 us
  Pallas kernels  62.9 us (81%)
  starting transfers between devices  13.1 us (17%)
  other arithmetic  1.17 us (2%)
    pallas_call x2, Pallas kernels, interior(): pl.pallas_call(functools.partial(interior_kernel, (begin, points)), name=...  44.5 us
    all_to_all x2, starting transfers between devices, exchange(): lax.all_to_all(payload, ('chip', 'cores'), split_axis=0, concat_axis=0, t...  13.1 us
    pallas_call x1, Pallas kernels, shards(): pl.pallas_call(functools.partial(finish_kernel, (fields, per_device, capa...  7.51 us
    pallas_call x1, Pallas kernels, shards(): pl.pallas_call(functools.partial(pack_kernel, (fields, per_device, capaci...  6.65 us
    pallas_call x1, Pallas kernels, shards(): pl.pallas_call(functools.partial(owner_kernel, (fields, per_device, capac...  4.28 us
  transfers between devices with their start and end apart: 2, of which 0 were waited for; matrix products, arithmetic and copies ran while one was open for 0% of the time, Pallas kernels for 57%

commit v1 on v0

v1 whole, which is shorter than its diff:
```python
import functools

import jax
import jax.numpy as jnp
from jax import lax
from jax.experimental import pallas as pl
from jax.experimental.pallas import tpu as pltpu
from jax.sharding import PartitionSpec as P

F32 = jnp.float32
BF16 = jnp.bfloat16
I32 = jnp.int32
EDGES = 4
LANES = 128
ROWS = 8
MIB = 1024 * 1024


def iota(shape, axis):
    return lax.broadcasted_iota(I32, shape, axis)


def halves(values):
    high = values.astype(BF16)
    low = (values - high.astype(F32)).astype(BF16)
    return high, low


def dot(left, right):
    return lax.dot_general(left, right, (((1,), (0,)), ((), ())), preferred_element_type=F32)


def dot_nt(left, right):
    return lax.dot_general(left, right, (((1,), (1,)), ((), ())), preferred_element_type=F32)


def lane_gather(values, index):
    return jnp.take_along_axis(values, index, axis=1)


class Codes:
    def __init__(self, per_device, points):
        self.bits = (points - 1).bit_length()
        self.local_bits = max(1, (per_device - 1).bit_length())
        self.mask = (1 << self.bits) - 1
        self.at_start = self.bits
        self.at_edge = 2 * self.bits
        self.at_local = self.at_edge + 2
        self.at_device = self.at_local + self.local_bits

    def pack(self, device, detail):
        return (
            (device << self.at_device)
            | (detail[0] << self.at_local)
            | (detail[1] << self.at_edge)
            | (detail[2] << self.at_start)
            | detail[3]
        )

    def length(self, code):
        return code & self.mask

    def start(self, code):
        return (code >> self.at_start) & self.mask

    def edge(self, code):
        return (code >> self.at_edge) & 3

    def local(self, code):
        return (code >> self.at_local) & ((1 << self.local_bits) - 1)

    def device(self, code):
        return code >> self.at_device


def side_codes(fields, device, detail):
    return fields.pack(device, [detail[i : i + 1, :] for i in range(4)])


def edge_row(fields, code):
    return fields.local(code) * EDGES + ((EDGES - fields.edge(code)) & (EDGES - 1))


def slot_tables(fields, code, me, owners, capacity):
    sides = code.shape[1] // owners
    slots = owners * capacity
    spread = jnp.concatenate(
        [
            jnp.broadcast_to(code[:, o * sides : (o + 1) * sides], (capacity, sides))
            for o in range(owners)
        ],
        axis=0,
    )
    mine = fields.device(spread) == me
    earlier = (iota((sides, sides), 0) < iota((sides, sides), 1)).astype(F32).astype(BF16)
    rank = dot(mine.astype(F32).astype(BF16), earlier).astype(I32)
    wanted = iota((slots, sides), 0) % capacity
    value = (fields.start(spread) << 16) | (edge_row(fields, spread) + 1)
    chosen = jnp.where(mine & (rank == wanted), value.astype(F32), 0.0)
    found = jnp.sum(chosen, axis=1, keepdims=True).astype(I32)
    return (found & 0xFFFF) - 1, found >> 16


def fold_window(tiles, last_pieces, window):
    lane = iota(tiles[0].shape, 1)
    out = []
    for at in range(5):
        if at < 4:
            out.append(jnp.where(lane < window, tiles[at], last_pieces[at]))
        else:
            out.append(tiles[at])
    return out


def unfold_last(tiles, window):
    quarter = window // 4
    lane = iota(tiles[0].shape, 1)
    lanes = tiles[0].shape[1]
    value = None
    for at in range(4):
        shift = (lanes - (window - quarter * at)) % lanes
        piece = pltpu.roll(tiles[at], shift, 1)
        value = piece if value is None else jnp.where(lane >= quarter * at, piece, value)
    return value


def pack_kernel(
    cfg, me_ref, device_ref, detail_ref, field_ref, out_ref, held_ref, strips_ref, arrival
):
    fields, owners, per_device, capacity, window, batch, points = cfg
    edges = EDGES * per_device
    slots = owners * capacity
    loads = []
    for patch in range(per_device):
        loads.append(
            pltpu.make_async_copy(field_ref.at[patch], held_ref.at[patch], arrival.at[patch])
        )
        loads[-1].start()

    code = side_codes(fields, device_ref[...], detail_ref)
    row, start = slot_tables(fields, code, me_ref[0], owners, capacity)
    picker = jnp.where(iota((slots, 2 * edges), 1) % edges == row, 1.0, 0.0).astype(BF16)
    base = iota((slots, points), 1) + start - 1

    lane = iota((points, points), 1)
    rows = EDGES * batch
    sub = iota((rows, points), 0)
    for step in range(per_device // batch):
        columns = jnp.zeros((points, points), F32)
        for b in range(batch):
            patch = step * batch + b
            loads[patch].wait()
            for c in range(6):
                at = EDGES * (c * batch + b)
                moved = pltpu.roll(held_ref[patch, c], (2 + at) % points, 1)
                columns = jnp.where((lane >= at) & (lane < at + EDGES), moved, columns)
        other = jnp.where(
            lane % EDGES == 1, pltpu.roll(columns, 1, 1), pltpu.roll(columns, points - 1, 1)
        )
        turned = jnp.transpose(1.5 * columns - 0.5 * other)
        for c in range(6):
            block = turned[c * rows : (c + 1) * rows]
            for b in range(batch):
                patch = step * batch + b
                top = 1.5 * held_ref[patch, c, 0:1, :] - 0.5 * held_ref[patch, c, 1:2, :]
                bottom = (
                    1.5 * held_ref[patch, c, points - 1 : points, :]
                    - 0.5 * held_ref[patch, c, points - 2 : points - 1, :]
                )
                block = jnp.where(sub == EDGES * b, top, block)
                block = jnp.where(sub == EDGES * b + 3, bottom, block)
            strips_ref[c, step * rows : (step + 1) * rows, :] = block

    high, low = halves(jnp.concatenate([strips_ref[c] for c in range(6)], axis=1))
    picked = dot(picker, jnp.concatenate([high, low], axis=0))
    quarter = window // 4
    tiles = [
        lane_gather(picked[:, c * points : (c + 1) * points], base & (points - 1))
        for c in range(5)
    ]
    last = picked[:, 5 * points :]
    pieces = [
        lane_gather(last, (base - (window - quarter * at)) & (points - 1)) for at in range(4)
    ]
    for at, tile in enumerate(fold_window(tiles, pieces, window)):
        out_ref[:, at * capacity : (at + 1) * capacity, :] = tile.reshape(owners, capacity, points)


def read_slots(ref, capacity, window):
    owners, rows, lanes = ref.shape
    tiles = [
        ref[:, at * capacity : (at + 1) * capacity, :].reshape(owners * capacity, lanes)
        for at in range(5)
    ]
    tiles.append(unfold_last(tiles, window))
    return tiles


def tables_kernel(
    cfg,
    me_ref,
    device_ref,
    detail_ref,
    angle_ref,
    gather_ref,
    start_ref,
    taker_ref,
    giver_ref,
    centre_ref,
    near_ref,
    opening_ref,
    spread_ref,
    frame_ref,
):
    fields, owners, per_device, capacity, points = cfg
    edges = EDGES * per_device
    slots = owners * capacity
    sides = device_ref.shape[1] // owners
    owned = sides // 2
    me = me_ref[0]
    code = side_codes(fields, device_ref[...], detail_ref)
    row, start = slot_tables(fields, code, me, owners, capacity)
    picker = jnp.where(iota((slots, 2 * edges), 1) % edges == row, 1.0, 0.0)
    gather = jnp.transpose(picker)[:edges].astype(BF16)
    gather_ref[...] = jnp.concatenate([gather, gather], axis=1)
    start_ref[...] = jnp.broadcast_to(start, (slots, points))

    own = pl.ds(pl.multiple_of(me * sides, sides), sides)
    own_code = fields.pack(device_ref[:, own], [detail_ref[i : i + 1, own] for i in range(4)])
    code_row = jnp.broadcast_to(own_code, (sides, sides))
    code = jnp.transpose(code_row)
    device, device_row = fields.device(code), fields.device(code_row)
    same = device == device_row
    sub, lane = iota((sides, sides), 0), iota((sides, sides), 1)
    rank = jnp.sum(jnp.where(same & (lane < sub), 1.0, 0.0), axis=1, keepdims=True).astype(I32)
    rank_row = jnp.sum(jnp.where(same & (sub < lane), 1.0, 0.0), axis=0, keepdims=True).astype(I32)
    slot = device[:, 0:1] * capacity + rank
    slot_row = device_row[0:1] * capacity + rank_row
    taker_ref[...] = jnp.where(iota((sides, 2 * slots), 1) % slots == slot, 1.0, 0.0).astype(BF16)
    giver = jnp.where(iota((slots, sides), 0) == slot_row, 1.0, 0.0).astype(BF16)
    giver_ref[...] = jnp.concatenate([giver, giver], axis=1)

    start = fields.start(code)
    length = fields.length(code).astype(F32)
    quad = iota((sides, points), 1)
    param = (quad.astype(F32) + 0.5) * length * (1.0 / points)
    centre = (param + 0.5).astype(I32)
    offset = param - centre.astype(F32)
    centre_ref[...] = centre
    near_ref[0] = jnp.where(start + centre >= 1, 0.5 * jnp.square(0.5 - offset), 0.0)
    near_ref[1] = 0.75 - offset * offset
    near_ref[2] = jnp.where(start + centre + 1 < points, 0.5 * jnp.square(0.5 + offset), 0.0)
    opening = jnp.ceil((quad.astype(F32) - 0.5) * (float(points) / length) - 0.501).astype(I32)
    opening_ref[...] = opening
    for m in range(2):
        at = opening + m
        offset = (at.astype(F32) + 0.5) * length * (1.0 / points) - quad.astype(F32)
        inside = (at >= 0) & (at < points) & (offset >= -0.5) & (offset < 0.5)
        spread_ref[3 * m] = jnp.where(
            inside & (start + quad >= 1), 0.5 * jnp.square(0.5 - offset), 0.0
        )
        spread_ref[3 * m + 1] = jnp.where(inside, 0.75 - offset * offset, 0.0)
        spread_ref[3 * m + 2] = jnp.where(
            inside & (start + quad + 1 < points), 0.5 * jnp.square(0.5 + offset), 0.0
        )

    cosine, sine = jnp.cos(angle_ref[...]), jnp.sin(angle_ref[...])
    cos_a, cos_b, cos_g = [cosine[i : i + 1] for i in range(3)]
    sin_a, sin_b, sin_g = [sine[i : i + 1] for i in range(3)]
    entries = [
        cos_g * cos_b,
        cos_g * sin_b * sin_a - sin_g * cos_a,
        cos_g * sin_b * cos_a + sin_g * sin_a,
        sin_g * cos_b,
        sin_g * sin_b * sin_a + cos_g * cos_a,
        sin_g * sin_b * cos_a - cos_g * sin_a,
        -sin_b,
        cos_b * sin_a,
        cos_b * cos_a,
    ]
    for e, entry in enumerate(entries):
        frame_ref[e] = jnp.transpose(jnp.broadcast_to(entry, (points, owned)))


def owner_kernel(
    cfg,
    arrived_ref,
    penalty_ref,
    taker_ref,
    giver_ref,
    centre_ref,
    near_ref,
    opening_ref,
    spread_ref,
    frame_ref,
    out_ref,
    work_ref,
):
    owners, capacity, window, points = cfg
    sides = taker_ref.shape[0]
    owned = sides // 2
    tiles = jnp.concatenate(read_slots(arrived_ref, capacity, window), axis=1)
    high, low = halves(tiles)
    taken = dot(taker_ref[...], jnp.concatenate([high, low], axis=0))
    centre = centre_ref[...]
    for c in range(6):
        values = taken[:, c * points : (c + 1) * points]
        work_ref[c] = (
            near_ref[0] * lane_gather(values, centre)
            + near_ref[1] * lane_gather(values, centre + 1)
            + near_ref[2] * lane_gather(values, (centre + 2) & (points - 1))
        )

    for b in range(2):
        ahead = [work_ref[3 * b + c, pl.ds(0, owned, stride=2), :] for c in range(3)]
        behind = [work_ref[3 * b + c, pl.ds(1, owned, stride=2), :] for c in range(3)]
        weight = penalty_ref[b]
        loads = [
            weight
            * (
                ahead[c]
                - (
                    frame_ref[3 * c] * behind[0]
                    + frame_ref[3 * c + 1] * behind[1]
                    + frame_ref[3 * c + 2] * behind[2]
                )
            )
            for c in range(3)
        ]
        for c in range(3):
            work_ref[3 * b + c, pl.ds(0, owned, stride=2), :] = loads[c]
            work_ref[3 * b + c, pl.ds(1, owned, stride=2), :] = -(
                frame_ref[c] * loads[0]
                + frame_ref[3 + c] * loads[1]
                + frame_ref[6 + c] * loads[2]
            )

    opening = opening_ref[...]
    forces = []
    for c in range(6):
        loads = work_ref[c]
        one = lane_gather(loads, opening & (points - 1))
        two = lane_gather(loads, (opening + 1) & (points - 1))
        force = spread_ref[0] * one + spread_ref[3] * two
        for d in range(1, 3):
            force = force + pltpu.roll(spread_ref[d] * one + spread_ref[3 + d] * two, d, 1)
        forces.append(force)
    high, low = halves(jnp.concatenate(forces, axis=1))
    given = dot(giver_ref[...], jnp.concatenate([high, low], axis=0))
    tiles = [given[:, c * points : (c + 1) * points] for c in range(5)]
    last = given[:, 5 * points :]
    quarter = window // 4
    pieces = [pltpu.roll(last, window - quarter * at, 1) for at in range(4)]
    for at, tile in enumerate(fold_window(tiles, pieces, window)):
        out_ref[:, at * capacity : (at + 1) * capacity, :] = tile.reshape(owners, capacity, points)


def interior_patch(points, weight, field_ref, table_ref, out_ref, applied_ref, mixed_ref):
    left = table_ref[0:3].reshape(3 * points, points)
    left_high, left_low = halves(left)
    field_high, field_low = [], []
    for c in range(6):
        high, low = halves(field_ref[c])
        field_high.append(high)
        field_low.append(low)
    field_high = jnp.concatenate(field_high, axis=1)
    field_low = jnp.concatenate(field_low, axis=1)
    applied_ref[...] = dot(
        jnp.concatenate([left_high, left_low], axis=1),
        jnp.concatenate([field_high, field_high], axis=0),
    ) + dot(left_high, field_low)

    chunk = points // 2
    groups = (((0, 0), (3, 1), (4, 2)), ((1, 1),), ((2, 2),))
    for at in range(points // chunk):
        for c in range(6):
            for g, terms in enumerate(groups):
                total = None
                for t, m in terms:
                    for d in range(6):
                        value = (
                            weight(t, c, d)
                            * applied_ref[
                                m * points + at * chunk : m * points + (at + 1) * chunk,
                                d * points : (d + 1) * points,
                            ]
                        )
                        total = value if total is None else total + value
                high, low = halves(total)
                rows = slice(c * points + at * chunk, c * points + (at + 1) * chunk)
                mixed_ref[rows, g * points : (g + 1) * points] = high
                mixed_ref[rows, (3 + g) * points : (4 + g) * points] = low

    right = jnp.concatenate([table_ref[4], table_ref[3], table_ref[5]], axis=1)
    right_high, right_low = halves(right)
    right = jnp.concatenate([right_high, right_low], axis=0)
    both = dot_nt(mixed_ref[...], jnp.concatenate([right, right], axis=1))
    total = both[:, :points] + both[:, points:]
    out_ref[...] = total.reshape(6, points, points)


def interior_kernel(cfg, coupling_ref, field_ref, table_ref, out_ref, applied_ref, mixed_ref):
    first, batch, points = cfg
    for b in range(batch):
        local = pl.program_id(0) * batch + b
        patch = first + local

        def weight(t, c, d):
            return coupling_ref[patch, (t * 6 + c) * 6 + d]

        interior_patch(
            points,
            weight,
            field_ref.at[b],
            table_ref.at[b],
            out_ref.at[b],
            applied_ref.at[b],
            mixed_ref.at[b],
        )


def finish_kernel(
    cfg,
    gather_ref,
    start_ref,
    arrived_ref,
    first_ref,
    second_ref,
    out_ref,
    held_ref,
    edge_ref,
    turned_ref,
    arrival,
    leaving,
):
    per_device, capacity, window, batch, points = cfg
    edges = EDGES * per_device
    steps = per_device // batch
    half = steps // 2
    loads, stores = [], []
    for step in range(steps):
        source = first_ref if step < half else second_ref
        block = pl.ds(step % half * batch, batch)
        own = held_ref.at[pl.ds(step * batch, batch)]
        loads.append(pltpu.make_async_copy(source.at[block], own, arrival.at[step]))
        loads[-1].start()
        stores.append(
            pltpu.make_async_copy(own, out_ref.at[pl.ds(step * batch, batch)], leaving.at[step])
        )

    at = iota(start_ref.shape, 1) - start_ref[...] + 1
    valid = (at >= 0) & (at < window)
    index = at & (points - 1)
    tiles = [
        jnp.where(valid, lane_gather(tile, index), 0.0)
        for tile in read_slots(arrived_ref, capacity, window)
    ]
    high, low = halves(jnp.concatenate(tiles, axis=1))
    total = dot(gather_ref[...], jnp.concatenate([high, low], axis=0))
    for c in range(6):
        part = total[:, c * points : (c + 1) * points]
        edge_ref[c] = part
        high = part.astype(BF16).astype(F32)
        both = jnp.concatenate([high, part - high], axis=0)
        turned_ref[c * points : (c + 1) * points, :] = jnp.transpose(both).astype(BF16)

    width = batch * points
    kk = iota((2 * edges, width), 0) % edges
    at = iota((2 * edges, width), 1)
    lane = at % points
    which = kk % EDGES
    near = lane == jnp.where(which == 1, points - 1, jnp.where(which == 2, 0, -1))
    next_to = lane == jnp.where(which == 1, points - 2, jnp.where(which == 2, 1, -1))
    weight = jnp.where(near, 1.5, jnp.where(next_to, -0.5, 0.0))
    ahead = kk // EDGES - at // points
    sub = iota((ROWS, points), 0)
    for step in range(steps):
        select = jnp.where(ahead == step * batch, weight, 0.0).astype(BF16)
        add = dot(turned_ref[...], select)
        loads[step].wait()
        for b in range(batch):
            patch = step * batch + b
            for c in range(6):
                value = held_ref[patch, c]
                value = value + add[c * points : (c + 1) * points, b * points : (b + 1) * points]
                top = edge_ref[c, EDGES * patch : EDGES * patch + 1, :]
                bottom = edge_ref[c, EDGES * patch + 3 : EDGES * patch + 4, :]
                held_ref[patch, c, 0:ROWS] = value[0:ROWS] + jnp.where(
                    sub == 0, 1.5 * top, jnp.where(sub == 1, -0.5 * top, 0.0)
                )
                held_ref[patch, c, ROWS : points - ROWS] = value[ROWS : points - ROWS]
                held_ref[patch, c, points - ROWS :] = value[points - ROWS :] + jnp.where(
                    sub == ROWS - 1, 1.5 * bottom, jnp.where(sub == ROWS - 2, -0.5 * bottom, 0.0)
                )
        stores[step].start()
    for store in stores:
        store.wait()


def exchange(payload):
    return lax.all_to_all(payload, ("chip", "cores"), split_axis=0, concat_axis=0, tiled=True)


def whole(shape):
    return pl.BlockSpec(shape, lambda *_: (0,) * len(shape))


def in_hbm(value):
    return pltpu.with_memory_space_constraint(value, pltpu.HBM)


def params(mib):
    return pltpu.CompilerParams(vmem_limit_bytes=mib * MIB)


def shards(patch_field, patch_tables, coupling, side_device, side_detail, penalty, angles):
    devices = lax.axis_size(("chip", "cores"))
    me = lax.axis_index(("chip", "cores")).astype(I32).reshape(1)
    per_device, _, points, _ = patch_field.shape
    owned = penalty.shape[0]
    sides = 2 * owned
    capacity = -(-max(2, 2 * sides // devices) // ROWS) * ROWS
    slots = devices * capacity
    edges = EDGES * per_device
    window = 3 * points // 4 + 4
    fields = Codes(per_device, points)
    smem = pl.BlockSpec(memory_space=pltpu.SMEM)
    vmem = pl.BlockSpec(memory_space=pltpu.VMEM)
    patch_field, patch_tables = in_hbm(patch_field), in_hbm(patch_tables)
    device_row = side_device.reshape(1, -1)
    detail_rows = side_detail.T
    payload_shape = (devices, 5 * capacity, points)
    payload = pltpu.HBM(payload_shape, F32)
    coupling = coupling.reshape(per_device, -1)
    weights = in_hbm(jnp.swapaxes(penalty, 0, 1))

    batch = 4
    outgoing = pl.pallas_call(
        functools.partial(
            pack_kernel, (fields, devices, per_device, capacity, window, batch, points)
        ),
        name="pack",
        out_shape=payload,
        grid=(1,),
        in_specs=[
            smem,
            whole(device_row.shape),
            whole(detail_rows.shape),
            pl.BlockSpec(memory_space=pl.ANY),
        ],
        out_specs=whole(payload_shape),
        scratch_shapes=[
            pltpu.VMEM(patch_field.shape, F32),
            pltpu.VMEM((6, edges, points), F32),
            pltpu.SemaphoreType.DMA((per_device,)),
        ],
        compiler_params=params(56),
    )(me, device_row, detail_rows, patch_field)
    arrived = exchange(outgoing)

    def tied(value, after):
        return lax.optimization_barrier((value, after))[0]

    def table(shape, kind):
        return jax.ShapeDtypeStruct(shape, kind)

    tables = pl.pallas_call(
        functools.partial(tables_kernel, (fields, devices, per_device, capacity, points)),
        name="tables",
        out_shape=[
            table((edges, 2 * slots), BF16),
            table((slots, points), I32),
            table((sides, 2 * slots), BF16),
            table((slots, 2 * sides), BF16),
            table((sides, points), I32),
            table((3, sides, points), F32),
            table((sides, points), I32),
            table((6, sides, points), F32),
            table((9, owned, points), F32),
        ],
        in_specs=[smem] + [vmem] * 3,
        out_specs=[vmem] * 9,
        compiler_params=params(56),
    )(tied(me, outgoing), device_row, detail_rows, angles.T)
    tables = [in_hbm(value) for value in tables]
    gather, start_table = tables[:2]

    def interior(begin, end, after):
        count = end - begin
        step = 2
        block = pl.BlockSpec((step, 6, points, points), lambda i: (i + begin // step, 0, 0, 0))
        shape = (count,) + patch_field.shape[1:]
        return pl.pallas_call(
            functools.partial(interior_kernel, (begin, step, points)),
            name="interior",
            out_shape=pltpu.HBM(shape, F32),
            grid=(count // step,),
            in_specs=[smem, block, block],
            out_specs=pl.BlockSpec((step, 6, points, points), lambda i: (i, 0, 0, 0)),
            scratch_shapes=[
                pltpu.VMEM((step, 3 * points, 6 * points), F32),
                pltpu.VMEM((step, 6 * points, 6 * points), BF16),
            ],
            compiler_params=params(48),
            cost_estimate=pl.CostEstimate(
                flops=count * 6 * 6 * 6 * points**3,
                bytes_accessed=count * 18 * points * points * 4,
                transcendentals=0,
            ),
        )(tied(coupling, after), patch_field, patch_tables)

    half = per_device // 2
    first = interior(0, half, outgoing)
    weights = tied(weights, first)
    back = pl.pallas_call(
        functools.partial(owner_kernel, (devices, capacity, window, points)),
        name="owner",
        out_shape=payload,
        grid=(1,),
        in_specs=[whole(payload_shape), whole(weights.shape)] + [whole(t.shape) for t in tables[2:]],
        out_specs=whole(payload_shape),
        scratch_shapes=[pltpu.VMEM((6, sides, points), F32)],
        compiler_params=params(40),
    )(arrived, weights, *tables[2:])
    returned = exchange(back)
    second = interior(half, per_device, back)
    gather = tied(gather, second)

    batch = 2
    anywhere = pl.BlockSpec(memory_space=pl.ANY)
    return pl.pallas_call(
        functools.partial(finish_kernel, (per_device, capacity, window, batch, points)),
        name="finish",
        out_shape=jax.ShapeDtypeStruct(patch_field.shape, F32),
        grid=(1,),
        in_specs=[
            whole(gather.shape),
            whole(start_table.shape),
            whole(payload_shape),
            anywhere,
            anywhere,
        ],
        out_specs=anywhere,
        scratch_shapes=[
            pltpu.VMEM(patch_field.shape, F32),
            pltpu.VMEM((6, edges, points), F32),
            pltpu.VMEM((6 * points, 2 * edges), BF16),
            pltpu.SemaphoreType.DMA((per_device // batch,)),
            pltpu.SemaphoreType.DMA((per_device // batch,)),
        ],
        compiler_params=params(60),
    )(gather, start_table, returned, first, second)


def solution(mesh):
    return jax.shard_map(
        shards,
        mesh=mesh,
        in_specs=(
            P(("chip", "cores"), None, None, None),
            P(("chip", "cores"), None, None, None),
            P(("chip", "cores"), None, None, None),
            P(),
            P(),
            P(("chip", "cores"), None, None),
            P(("chip", "cores"), None),
        ),
        out_specs=P(("chip", "cores"), None, None, None),
        check_vma=False,
    )
```

time: 77.9 us -> 69.7 us (0.89)
  Pallas kernels: 62.9 us -> 52.9 us
  waiting for transfers between devices: 0.01 us -> 1.35 us
  local copies, waits for them, and re-layouts: 0.28 us -> 1.61 us
  other arithmetic: 1.17 us -> 0 us
    pallas_call x5 -> x6, Pallas kernels: 62.9 us -> 52.9 us  [the longest x2 32.6 us: interior(): pl.pallas_call(functools.partial(interior_kernel, (begin, step, points)),...]
    unnamed x7, local copies, waits for them, and re-layouts: 0.02 us -> 1.48 us
    all_to_all x2, waiting for transfers between devices: 0.01 us -> 1.35 us  [exchange(): lax.all_to_all(payload, ('chip', 'cores'), split_axis=0, concat_axis=0, t...]
    or x1 -> x0, other arithmetic: 1.06 us -> none  [pack(): device << self.at_device | detail[..., 0] << self.at_local]
  transfers between devices with their start and end apart: 2 -> 2, of which waited for: 0 -> 1; matrix products, arithmetic and copies ran while one was open for 0% -> 1% of each run, Pallas kernels for 57% -> 50%
where the time goes in v1:
time: 69.7 us; the launch traced here: 69.3 us
  Pallas kernels  52.9 us (76%)
  starting transfers between devices  13.3 us (19%)
  local copies, waits for them, and re-layouts  1.61 us (2%)
  waiting for transfers between devices  1.35 us (2%)
    pallas_call x2, Pallas kernels, interior(): pl.pallas_call(functools.partial(interior_kernel, (begin, step, points)),...  32.6 us
    all_to_all x2, starting transfers between devices, exchange(): lax.all_to_all(payload, ('chip', 'cores'), split_axis=0, concat_axis=0, t...  13.3 us
    pallas_call x1, Pallas kernels, shards(): pl.pallas_call(functools.partial(pack_kernel, (fields, devices, per_devic...  7.15 us
    pallas_call x1, Pallas kernels, shards(): pl.pallas_call(functools.partial(finish_kernel, (per_device, capacity, wi...  6.11 us
    pallas_call x1, Pallas kernels, shards(): pl.pallas_call(functools.partial(owner_kernel, (devices, capacity, window...  4.66 us
    pallas_call x1, Pallas kernels, shards(): pl.pallas_call(functools.partial(tables_kernel, (fields, devices, per_dev...  2.31 us
    unnamed x7, local copies, waits for them, and re-layouts  1.48 us
  transfers between devices with their start and end apart: 2, of which 1 were waited for; matrix products, arithmetic and copies ran while one was open for 1% of the time, Pallas kernels for 50%

profile of v1, /device:TPU:0, one launch (start us, length us, event | category | flops | bytes accessed | tf_op | source)
XLA Modules:
  0.0 69.3 jit_solution(15860305592521635427)
XLA Ops:
  0.0 0.0 copy-start.2
  0.0 0.0 copy-start.1
  0.0 7.1 %pack.1 = f32[32,40,128]{2,1,0:T(8,128)} custom-call(s32[1]{0:T(128)} %bitcast.me_ref, s32[1,4096]{1,0:T(1,128)} %bitcast.12, s32[4,4096]{1,0:T(4,128)} %bitcast.9, f32[16,6,128,128]{3,2,1,0:T(8,128)} %field_ref.5), custom_call_target="tpu_custom_call" | custom-call | tf_op jit(solution)/shard_map/pack/pallas_call | solution.py:538
  7.2 7.3 %all-to-all-start = ((f32[32,40,128]{2,1,0:T(8,128)}), f32[32,40,128]{2,1,0:T(8,128)S(1)}, u32[]{:S(2)}, u32[]{:S(2)}) async-start(f32[32,40,128]{2,1,0:T(8,128)} %pack.1), calls=%async_computation | async-start | bytes 1310720 | tf_op jit(solution)/shard_map/all_to_all | solution.py:501
  14.5 0.0 copy-done.2
  14.5 0.6 copy.14
  15.1 0.0 copy-done.1
  15.1 0.1 copy.11.coupling_ref
  15.2 16.3 %interior.2.first_ref = f32[8,6,128,128]{3,2,1,0:T(8,128)} custom-call(f32[16,180]{1,0:T(8,128)S(1)} %copy.11.coupling_ref, f32[16,6,128,128]{3,2,1,0:T(8,128)} %field_ref.5, f32[16,6,128,128]{3,2,1,0:T(8,128)} %table_ref.3), custom_call_target="tpu_custom_call" | custom-call | flops 3623878656 | bytes 9437184 | tf_op jit(solution)/shard_map/interior/pallas_call | solution.py:593
  31.5 2.3 %tables.1 = (bf16[64,512]{1,0:T(8,128)(2,1)}, s32[256,128]{1,0:T(8,128)}, bf16[128,512]{1,0:T(8,128)(2,1)}, bf16[256,256]{1,0:T(8,128)(2,1)}, s32[128,128]{1,0:T...) custom-call(s32[1]{0:T(128)} %bitcast.me_ref, ...), custom_call_target="tpu_custom_call" | custom-call | tf_op jit(solution)/shard_map/tables/pallas_call | solution.py:567
  33.8 0.0 all-to-all-done.arrived_ref
  33.8 4.7 %owner.1 = f32[32,40,128]{2,1,0:T(8,128)} custom-call(f32[32,40,128]{2,1,0:T(8,128)S(1)} %all-to-all-done.arrived_ref, f32[2,64,128]{2,1,0:T(8,128)} %bitcast.11, bf16[128,512]{1,0:T(8,128)(2,1)} %get-tuple-element.23.taker_ref, bf16[256,256]{1,0:T(8,128)(2,1)} %get-tuple-element.24.giver_ref, s32[128,128]{1,0:T(8,128)} %get-tuple-element.25.centre_ref, ...), custom_call_target="tpu_custom_call" | custom-call | tf_op jit(solution)/shard_map/owner/pallas_call | solution.py:615
  38.5 6.0 %all-to-all-start.1 = ((f32[32,40,128]{2,1,0:T(8,128)}), f32[32,40,128]{2,1,0:T(8,128)S(1)}, u32[]{:S(2)}, u32[]{:S(2)}) async-start(f32[32,40,128]{2,1,0:T(8,128)} %owner.1), calls=%async_computation.1 | async-start | bytes 1310720 | tf_op jit(solution)/shard_map/all_to_all | solution.py:501
  44.5 0.1 copy.12.coupling_ref
  44.5 16.3 %interior.3.second_ref = f32[8,6,128,128]{3,2,1,0:T(8,128)} custom-call(f32[16,180]{1,0:T(8,128)S(1)} %copy.12.coupling_ref, f32[16,6,128,128]{3,2,1,0:T(8,128)} %field_ref.5, f32[16,6,128,128]{3,2,1,0:T(8,128)} %table_ref.3), custom_call_target="tpu_custom_call" | custom-call | flops 3623878656 | bytes 9437184 | tf_op jit(solution)/shard_map/interior/pallas_call | solution.py:593
  60.9 1.4 %all-to-all-done.1.arrived_ref = f32[32,40,128]{2,1,0:T(8,128)S(1)} async-done(((f32[32,40,128]{2,1,0:T(8,128)}), f32[32,40,128]{2,1,0:T(8,128)S(1)}, u32[]{:S(2)}, u32[]{:S(2)}) %all-to-all-start.1) | async-done | bytes 655392 | tf_op jit(solution)/shard_map/all_to_all | solution.py:501
  62.2 0.0 copy-start
  62.2 0.8 %copy-done = f32[32,40,128]{2,1,0:T(8,128)} copy-done((f32[32,40,128]{2,1,0:T(8,128)}, f32[32,40,128]{2,1,0:T(8,128)S(1)}, u32[]{:S(2)}) %copy-start) | copy-done | bytes 655384
  63.1 6.1 %finish.1 = f32[16,6,128,128]{3,2,1,0:T(8,128)} custom-call(bf16[64,512]{1,0:T(8,128)(2,1)} %get-tuple-element.31.gather_ref, s32[256,128]{1,0:T(8,128)} %get-tuple-element.32.start_ref, f32[32,40,128]{2,1,0:T(8,128)} %copy-done, f32[8,6,128,128]{3,2,1,0:T(8,128)} %interior.2.first_ref, f32[8,6,128,128]{3,2,1,0:T(8,128)} %interior.3.second_ref), custom_call_target="tpu_custom_call" | custom-call | tf_op jit(solution)/shard_map/finish/pallas_call | solution.py:631
  (1 shorter events, 0.0 us)
Async XLA Ops:
  0.0 14.5 %copy-start.2 = (f32[64,2,128]{2,1,0:T(2,128)S(1)}, f32[64,2,128]{2,1,0:T(2,128)}, u32[]{:S(2)}) copy-start(f32[64,2,128]{2,1,0:T(2,128)} %param.12) | copy-start | bytes 196612
  0.0 15.1 %copy-start.1 = (f32[16,5,6,6]{0,3,2,1:T(8,128)S(1)}, f32[16,5,6,6]{0,3,2,1:T(8,128)}, u32[]{:S(2)}) copy-start(f32[16,5,6,6]{0,3,2,1:T(8,128)} %param.9) | copy-start | bytes 34564
  7.2 26.6 %all-to-all-start = ((f32[32,40,128]{2,1,0:T(8,128)}), f32[32,40,128]{2,1,0:T(8,128)S(1)}, u32[]{:S(2)}, u32[]{:S(2)}) async-start(f32[32,40,128]{2,1,0:T(8,128)} %pack.1), calls=%async_computation | async-start | bytes 1310720 | tf_op jit(solution)/shard_map/all_to_all | solution.py:501
  38.5 23.8 %all-to-all-start.1 = ((f32[32,40,128]{2,1,0:T(8,128)}), f32[32,40,128]{2,1,0:T(8,128)S(1)}, u32[]{:S(2)}, u32[]{:S(2)}) async-start(f32[32,40,128]{2,1,0:T(8,128)} %owner.1), calls=%async_computation.1 | async-start | bytes 1310720 | tf_op jit(solution)/shard_map/all_to_all | solution.py:501
  62.2 0.8 %copy-start = (f32[32,40,128]{2,1,0:T(8,128)}, f32[32,40,128]{2,1,0:T(8,128)S(1)}, u32[]{:S(2)}) copy-start(f32[32,40,128]{2,1,0:T(8,128)S(1)} %all-to-all-done.1.arrived_ref) | copy-start | bytes 1966084

commit v2 on v1

--- a/solution.py
+++ b/solution.py
@@ -355,68 +355,54 @@
         out_ref[:, at * capacity : (at + 1) * capacity, :] = tile.reshape(owners, capacity, points)
 
 
-def interior_patch(points, weight, field_ref, table_ref, out_ref, applied_ref, mixed_ref):
-    left = table_ref[0:3].reshape(3 * points, points)
-    left_high, left_low = halves(left)
-    field_high, field_low = [], []
-    for c in range(6):
-        high, low = halves(field_ref[c])
-        field_high.append(high)
-        field_low.append(low)
-    field_high = jnp.concatenate(field_high, axis=1)
-    field_low = jnp.concatenate(field_low, axis=1)
-    applied_ref[...] = dot(
-        jnp.concatenate([left_high, left_low], axis=1),
-        jnp.concatenate([field_high, field_high], axis=0),
-    ) + dot(left_high, field_low)
-
-    chunk = points // 2
-    groups = (((0, 0), (3, 1), (4, 2)), ((1, 1),), ((2, 2),))
-    for at in range(points // chunk):
+def interior_kernel(cfg, coupling_ref, _, field_ref, table_ref, out_ref, *work):
+    first, batch, points = cfg
+    applied, mixed = work[:batch], work[batch:]
+
+    def apply_left(b):
+        high, low = halves(table_ref[b, 0:3].reshape(3 * points, points))
+        parts = [halves(field_ref[b, c]) for c in range(6)]
+        field_high = jnp.concatenate([part[0] for part in parts], axis=1)
+        field_low = jnp.concatenate([part[1] for part in parts], axis=1)
+        applied[b][...] = dot(
+            jnp.concatenate([high, low], axis=1),
+            jnp.concatenate([field_high, field_high], axis=0),
+        ) + dot(high, field_low)
+
+    def mix(b):
+        patch = pl.program_id(0) * batch + b + first
+        groups = (((0, 0), (3, 1), (4, 2)), ((1, 1),), ((2, 2),))
         for c in range(6):
             for g, terms in enumerate(groups):
                 total = None
                 for t, m in terms:
                     for d in range(6):
-                        value = (
-                            weight(t, c, d)
-                            * applied_ref[
-                                m * points + at * chunk : m * points + (at + 1) * chunk,
-                                d * points : (d + 1) * points,
-                            ]
-                        )
+                        rows = slice(m * points, (m + 1) * points)
+                        cols = slice(d * points, (d + 1) * points)
+                        value = coupling_ref[patch, (t * 6 + c) * 6 + d] * applied[b][rows, cols]
                         total = value if total is None else total + value
                 high, low = halves(total)
-                rows = slice(c * points + at * chunk, c * points + (at + 1) * chunk)
-                mixed_ref[rows, g * points : (g + 1) * points] = high
-                mixed_ref[rows, (3 + g) * points : (4 + g) * points] = low
-
-    right = jnp.concatenate([table_ref[4], table_ref[3], table_ref[5]], axis=1)
-    right_high, right_low = halves(right)
-    right = jnp.concatenate([right_high, right_low], axis=0)
-    both = dot_nt(mixed_ref[...], jnp.concatenate([right, right], axis=1))
-    total = both[:, :points] + both[:, points:]
-    out_ref[...] = total.reshape(6, points, points)
-
-
-def interior_kernel(cfg, coupling_ref, field_ref, table_ref, out_ref, applied_ref, mixed_ref):
-    first, batch, points = cfg
+                rows = slice(c * points, (c + 1) * points)
+                mixed[b][rows, g * points : (g + 1) * points] = high
+                mixed[b][rows, (3 + g) * points : (4 + g) * points] = low
+
+    def apply_right(b):
+        high, low = halves(
+            jnp.concatenate([table_ref[b, 4], table_ref[b, 3], table_ref[b, 5]], axis=1)
+        )
+        right = jnp.concatenate([high, low], axis=0)
+        both = dot_nt(mixed[b][...], jnp.concatenate([right, right], axis=1))
+        total = both[:, :points] + both[:, points:]
+        out_ref[b] = total.reshape(6, points, points)
+
+    apply_left(0)
     for b in range(batch):
-        local = pl.program_id(0) * batch + b
-        patch = first + local
-
-        def weight(t, c, d):
-            return coupling_ref[patch, (t * 6 + c) * 6 + d]
-
-        interior_patch(
-            points,
-            weight,
-            field_ref.at[b],
-            table_ref.at[b],
-            out_ref.at[b],
-            applied_ref.at[b],
-            mixed_ref.at[b],
-        )
+        if b + 1 < batch:
+            apply_left(b + 1)
+        if b > 0:
+            apply_right(b - 1)
+        mix(b)
+    apply_right(batch - 1)
 
 
 def finish_kernel(
@@ -587,30 +573,27 @@
 
     def interior(begin, end, after):
         count = end - begin
-        step = 2
-        block = pl.BlockSpec((step, 6, points, points), lambda i: (i + begin // step, 0, 0, 0))
+        block = pl.BlockSpec((batch, 6, points, points), lambda i: (i + begin // batch, 0, 0, 0))
         shape = (count,) + patch_field.shape[1:]
         return pl.pallas_call(
-            functools.partial(interior_kernel, (begin, step, points)),
+            functools.partial(interior_kernel, (begin, batch, points)),
             name="interior",
             out_shape=pltpu.HBM(shape, F32),
-            grid=(count // step,),
-            in_specs=[smem, block, block],
-            out_specs=pl.BlockSpec((step, 6, points, points), lambda i: (i, 0, 0, 0)),
-            scratch_shapes=[
-                pltpu.VMEM((step, 3 * points, 6 * points), F32),
-                pltpu.VMEM((step, 6 * points, 6 * points), BF16),
-            ],
-            compiler_params=params(48),
+            grid=(count // batch,),
+            in_specs=[smem, smem, block, block],
+            out_specs=pl.BlockSpec((batch, 6, points, points), lambda i: (i, 0, 0, 0)),
+            scratch_shapes=[pltpu.VMEM((3 * points, 6 * points), F32)] * batch
+            + [pltpu.VMEM((6 * points, 6 * points), BF16)] * batch,
+            compiler_params=params(52),
             cost_estimate=pl.CostEstimate(
                 flops=count * 6 * 6 * 6 * points**3,
                 bytes_accessed=count * 18 * points * points * 4,
                 transcendentals=0,
             ),
-        )(tied(coupling, after), patch_field, patch_tables)
+        )(coupling, tied(me, after), patch_field, patch_tables)
 
     half = per_device // 2
-    first = interior(0, half, outgoing)
+    first = in_hbm(interior(0, half, outgoing))
     weights = tied(weights, first)
     back = pl.pallas_call(
         functools.partial(owner_kernel, (devices, capacity, window, points)),
@@ -623,7 +606,7 @@
         compiler_params=params(40),
     )(arrived, weights, *tables[2:])
     returned = exchange(back)
-    second = interior(half, per_device, back)
+    second = in_hbm(interior(half, per_device, back))
     gather = tied(gather, second)
 
     batch = 2
@@ -648,7 +631,7 @@
             pltpu.SemaphoreType.DMA((per_device // batch,)),
             pltpu.SemaphoreType.DMA((per_device // batch,)),
         ],
-        compiler_params=params(60),
+        compiler_params=params(40),
     )(gather, start_table, returned, first, second)
 
 

time: 69.7 us -> 66.6 us (0.956)
  Pallas kernels: 52.9 us -> 48.5 us
  waiting for transfers between devices: 1.35 us -> 4.25 us
  local copies, waits for them, and re-layouts: 1.61 us -> 0.71 us
  starting transfers between devices: 13.3 us -> 12.6 us
    pallas_call x2, Pallas kernels: 32.6 us -> 28.4 us  [interior(): pl.pallas_call(functools.partial(interior_kernel, (begin, batch, points))...]
    all_to_all x2, waiting for transfers between devices: 1.35 us -> 4.25 us  [exchange(): lax.all_to_all(payload, ('chip', 'cores'), split_axis=0, concat_axis=0, t...]
    unnamed x7 -> x5, local copies, waits for them, and re-layouts: 1.48 us -> 0.64 us
    all_to_all x2, starting transfers between devices: 13.3 us -> 12.6 us  [exchange(): lax.all_to_all(payload, ('chip', 'cores'), split_axis=0, concat_axis=0, t...]
  transfers between devices with their start and end apart: 2 -> 2, of which waited for: 1 -> 2; matrix products, arithmetic and copies ran while one was open for 1% -> 1% of each run, Pallas kernels for 50% -> 46%
where the time goes in v2:
time: 66.6 us; the launch traced here: 66.2 us
  Pallas kernels  48.5 us (73%)
  starting transfers between devices  12.6 us (19%)
  waiting for transfers between devices  4.25 us (6%)
  local copies, waits for them, and re-layouts  0.71 us (1%)
    pallas_call x2, Pallas kernels, interior(): pl.pallas_call(functools.partial(interior_kernel, (begin, batch, points))...  28.4 us
    all_to_all x2, starting transfers between devices, exchange(): lax.all_to_all(payload, ('chip', 'cores'), split_axis=0, concat_axis=0, t...  12.6 us
    pallas_call x1, Pallas kernels, shards(): pl.pallas_call(functools.partial(pack_kernel, (fields, devices, per_devic...  7.15 us
    pallas_call x1, Pallas kernels, shards(): pl.pallas_call(functools.partial(finish_kernel, (per_device, capacity, wi...  5.97 us
    pallas_call x1, Pallas kernels, shards(): pl.pallas_call(functools.partial(owner_kernel, (devices, capacity, window...  4.66 us
    all_to_all x2, waiting for transfers between devices, exchange(): lax.all_to_all(payload, ('chip', 'cores'), split_axis=0, concat_axis=0, t...  4.25 us
    pallas_call x1, Pallas kernels, shards(): pl.pallas_call(functools.partial(tables_kernel, (fields, devices, per_dev...  2.33 us
  transfers between devices with their start and end apart: 2, of which 2 were waited for; matrix products, arithmetic and copies ran while one was open for 1% of the time, Pallas kernels for 46%

profile of v2, /device:TPU:0, one launch (start us, length us, event | category | flops | bytes accessed | tf_op | source)
XLA Modules:
  0.0 66.2 jit_solution(9370361960008153358)
XLA Ops:
  0.0 0.0 copy-start.1
  0.0 0.0 copy-start
  0.0 7.1 %pack.1 = f32[32,40,128]{2,1,0:T(8,128)} custom-call(s32[1]{0:T(128)} %bitcast.me_ref._, s32[1,4096]{1,0:T(1,128)} %bitcast.12, s32[4,4096]{1,0:T(4,128)} %bitcast.9, f32[16,6,128,128]{3,2,1,0:T(8,128)} %field_ref.5), custom_call_target="tpu_custom_call" | custom-call | tf_op jit(solution)/shard_map/pack/pallas_call | solution.py:524
  7.2 7.3 %all-to-all-start = ((f32[32,40,128]{2,1,0:T(8,128)}), f32[32,40,128]{2,1,0:T(8,128)S(1)}, u32[]{:S(2)}, u32[]{:S(2)}) async-start(f32[32,40,128]{2,1,0:T(8,128)} %pack.1), calls=%async_computation | async-start | bytes 1310720 | tf_op jit(solution)/shard_map/all_to_all | solution.py:487
  14.5 0.0 copy-done.1
  14.5 0.6 copy.14
  15.1 0.0 copy-done
  15.1 0.1 copy.12.coupling_ref
  15.2 2.3 %tables.1 = (bf16[64,512]{1,0:T(8,128)(2,1)}, s32[256,128]{1,0:T(8,128)}, bf16[128,512]{1,0:T(8,128)(2,1)}, bf16[256,256]{1,0:T(8,128)(2,1)}, s32[128,128]{1,0:T...) custom-call(s32[1]{0:T(128)} %bitcast.me_ref._, ...), custom_call_target="tpu_custom_call" | custom-call | tf_op jit(solution)/shard_map/tables/pallas_call | solution.py:553
  17.5 14.2 %interior.2.first_ref = f32[8,6,128,128]{3,2,1,0:T(8,128)} custom-call(f32[16,180]{1,0:T(8,128)S(1)} %copy.12.coupling_ref, s32[1]{0:T(128)} %bitcast.me_ref._, f32[16,6,128,128]{3,2,1,0:T(8,128)} %field_ref.5, f32[16,6,128,128]{3,2,1,0:T(8,128)} %table_ref.3), custom_call_target="tpu_custom_call" | custom-call | flops 3623878656 | bytes 9437184 | tf_op jit(solution)/shard_map/interior/pallas_call | solution.py:578
  31.7 0.7 %all-to-all-done.arrived_ref = f32[32,40,128]{2,1,0:T(8,128)S(1)} async-done(((f32[32,40,128]{2,1,0:T(8,128)}), f32[32,40,128]{2,1,0:T(8,128)S(1)}, u32[]{:S(2)}, u32[]{:S(2)}) %all-to-all-start) | async-done | bytes 655392 | tf_op jit(solution)/shard_map/all_to_all | solution.py:487
  32.4 4.7 %owner.1 = f32[32,40,128]{2,1,0:T(8,128)} custom-call(f32[32,40,128]{2,1,0:T(8,128)S(1)} %all-to-all-done.arrived_ref, f32[2,64,128]{2,1,0:T(8,128)} %bitcast.11, bf16[128,512]{1,0:T(8,128)(2,1)} %get-tuple-element.21.taker_ref, bf16[256,256]{1,0:T(8,128)(2,1)} %get-tuple-element.22.giver_ref, s32[128,128]{1,0:T(8,128)} %get-tuple-element.23.centre_ref, ...), custom_call_target="tpu_custom_call" | custom-call | tf_op jit(solution)/shard_map/owner/pallas_call | solution.py:598
  37.0 5.3 %all-to-all-start.1 = ((f32[32,40,128]{2,1,0:T(8,128)}), f32[32,40,128]{2,1,0:T(8,128)S(1)}, u32[]{:S(2)}, u32[]{:S(2)}) async-start(f32[32,40,128]{2,1,0:T(8,128)} %owner.1), calls=%async_computation.1 | async-start | bytes 1310720 | tf_op jit(solution)/shard_map/all_to_all | solution.py:487
  42.4 14.2 %interior.3.second_ref = f32[8,6,128,128]{3,2,1,0:T(8,128)} custom-call(f32[16,180]{1,0:T(8,128)S(1)} %copy.12.coupling_ref, s32[1]{0:T(128)} %bitcast.me_ref._, f32[16,6,128,128]{3,2,1,0:T(8,128)} %field_ref.5, f32[16,6,128,128]{3,2,1,0:T(8,128)} %table_ref.3), custom_call_target="tpu_custom_call" | custom-call | flops 3623878656 | bytes 9437184 | tf_op jit(solution)/shard_map/interior/pallas_call | solution.py:578
  56.6 3.5 %all-to-all-done.1.arrived_ref = f32[32,40,128]{2,1,0:T(8,128)S(1)} async-done(((f32[32,40,128]{2,1,0:T(8,128)}), f32[32,40,128]{2,1,0:T(8,128)S(1)}, u32[]{:S(2)}, u32[]{:S(2)}) %all-to-all-start.1) | async-done | bytes 655392 | tf_op jit(solution)/shard_map/all_to_all | solution.py:487
  60.1 6.0 %finish.1 = f32[16,6,128,128]{3,2,1,0:T(8,128)} custom-call(bf16[64,512]{1,0:T(8,128)(2,1)} %get-tuple-element.29.gather_ref, s32[256,128]{1,0:T(8,128)} %get-tuple-element.30.start_ref, f32[32,40,128]{2,1,0:T(8,128)S(1)} %all-to-all-done.1.arrived_ref, f32[8,6,128,128]{3,2,1,0:T(8,128)} %interior.2.first_ref, f32[8,6,128,128]{3,2,1,0:T(8,128)} %interior.3.second_ref), custom_call_target="tpu_custom_call" | custom-call | tf_op jit(solution)/shard_map/finish/pallas_call | solution.py:614
  (1 shorter events, 0.0 us)
Async XLA Ops:
  0.0 14.5 %copy-start.1 = (f32[64,2,128]{2,1,0:T(2,128)S(1)}, f32[64,2,128]{2,1,0:T(2,128)}, u32[]{:S(2)}) copy-start(f32[64,2,128]{2,1,0:T(2,128)} %param.12) | copy-start | bytes 196612
  0.0 15.1 %copy-start = (f32[16,5,6,6]{0,3,2,1:T(8,128)S(1)}, f32[16,5,6,6]{0,3,2,1:T(8,128)}, u32[]{:S(2)}) copy-start(f32[16,5,6,6]{0,3,2,1:T(8,128)} %param.9) | copy-start | bytes 34564
  7.2 25.2 %all-to-all-start = ((f32[32,40,128]{2,1,0:T(8,128)}), f32[32,40,128]{2,1,0:T(8,128)S(1)}, u32[]{:S(2)}, u32[]{:S(2)}) async-start(f32[32,40,128]{2,1,0:T(8,128)} %pack.1), calls=%async_computation | async-start | bytes 1310720 | tf_op jit(solution)/shard_map/all_to_all | solution.py:487
  37.0 23.1 %all-to-all-start.1 = ((f32[32,40,128]{2,1,0:T(8,128)}), f32[32,40,128]{2,1,0:T(8,128)S(1)}, u32[]{:S(2)}, u32[]{:S(2)}) async-start(f32[32,40,128]{2,1,0:T(8,128)} %owner.1), calls=%async_computation.1 | async-start | bytes 1310720 | tf_op jit(solution)/shard_map/all_to_all | solution.py:487

commit v3 on v2

--- a/solution.py
+++ b/solution.py
@@ -295,14 +295,37 @@
     frame_ref,
     out_ref,
     work_ref,
+    *held,
 ):
     owners, capacity, window, points = cfg
-    sides = taker_ref.shape[0]
+    arrival = held[-1]
+    tables = {}
+    names = ("taker", "centre", "near", "penalty", "frame", "opening", "spread", "giver")
+    sources = (
+        taker_ref,
+        centre_ref,
+        near_ref,
+        penalty_ref,
+        frame_ref,
+        opening_ref,
+        spread_ref,
+        giver_ref,
+    )
+    for at, (name, source) in enumerate(zip(names, sources)):
+        tables[name] = (pltpu.make_async_copy(source, held[at], arrival.at[at]), held[at])
+        tables[name][0].start()
+
+    def ready(name):
+        tables[name][0].wait()
+        return tables[name][1]
+
+    sides = work_ref.shape[1]
     owned = sides // 2
     tiles = jnp.concatenate(read_slots(arrived_ref, capacity, window), axis=1)
     high, low = halves(tiles)
-    taken = dot(taker_ref[...], jnp.concatenate([high, low], axis=0))
-    centre = centre_ref[...]
+    taken = dot(ready("taker")[...], jnp.concatenate([high, low], axis=0))
+    centre = ready("centre")[...]
+    near_ref = ready("near")
     for c in range(6):
         values = taken[:, c * points : (c + 1) * points]
         work_ref[c] = (
@@ -311,6 +334,8 @@
             + near_ref[2] * lane_gather(values, (centre + 2) & (points - 1))
         )
 
+    penalty_ref = ready("penalty")
+    frame_ref = ready("frame")
     for b in range(2):
         ahead = [work_ref[3 * b + c, pl.ds(0, owned, stride=2), :] for c in range(3)]
         behind = [work_ref[3 * b + c, pl.ds(1, owned, stride=2), :] for c in range(3)]
@@ -335,7 +360,8 @@
                 + frame_ref[6 + c] * loads[2]
             )
 
-    opening = opening_ref[...]
+    opening = ready("opening")[...]
+    spread_ref = ready("spread")
     forces = []
     for c in range(6):
         loads = work_ref[c]
@@ -346,7 +372,7 @@
             force = force + pltpu.roll(spread_ref[d] * one + spread_ref[3 + d] * two, d, 1)
         forces.append(force)
     high, low = halves(jnp.concatenate(forces, axis=1))
-    given = dot(giver_ref[...], jnp.concatenate([high, low], axis=0))
+    given = dot(ready("giver")[...], jnp.concatenate([high, low], axis=0))
     tiles = [given[:, c * points : (c + 1) * points] for c in range(5)]
     last = given[:, 5 * points :]
     quarter = window // 4
@@ -548,7 +574,7 @@
         return lax.optimization_barrier((value, after))[0]
 
     def table(shape, kind):
-        return jax.ShapeDtypeStruct(shape, kind)
+        return pltpu.HBM(shape, kind)
 
     tables = pl.pallas_call(
         functools.partial(tables_kernel, (fields, devices, per_device, capacity, points)),
@@ -578,7 +604,7 @@
         return pl.pallas_call(
             functools.partial(interior_kernel, (begin, batch, points)),
             name="interior",
-            out_shape=pltpu.HBM(shape, F32),
+            out_shape=pltpu.HBM(shape, F32) if begin else jax.ShapeDtypeStruct(shape, F32),
             grid=(count // batch,),
             in_specs=[smem, smem, block, block],
             out_specs=pl.BlockSpec((batch, 6, points, points), lambda i: (i, 0, 0, 0)),
@@ -593,16 +619,19 @@
         )(coupling, tied(me, after), patch_field, patch_tables)
 
     half = per_device // 2
-    first = in_hbm(interior(0, half, outgoing))
+    first = interior(0, half, outgoing)
     weights = tied(weights, first)
+    taker, giver, centre, near, opening, spread, frame = tables[2:]
+    held = (taker, centre, near, weights, frame, opening, spread, giver)
     back = pl.pallas_call(
         functools.partial(owner_kernel, (devices, capacity, window, points)),
         name="owner",
         out_shape=payload,
-        grid=(1,),
-        in_specs=[whole(payload_shape), whole(weights.shape)] + [whole(t.shape) for t in tables[2:]],
-        out_specs=whole(payload_shape),
-        scratch_shapes=[pltpu.VMEM((6, sides, points), F32)],
+        in_specs=[vmem] + [pl.BlockSpec(memory_space=pl.ANY)] * 8,
+        out_specs=vmem,
+        scratch_shapes=[pltpu.VMEM((6, sides, points), F32)]
+        + [pltpu.VMEM(t.shape, t.dtype) for t in held]
+        + [pltpu.SemaphoreType.DMA((len(held),))],
         compiler_params=params(40),
     )(arrived, weights, *tables[2:])
     returned = exchange(back)
@@ -619,7 +648,7 @@
         in_specs=[
             whole(gather.shape),
             whole(start_table.shape),
-            whole(payload_shape),
+            vmem,
             anywhere,
             anywhere,
         ],

time: 66.6 us -> 67 us (level)
  no operation moved by 1% of the time
where the time goes in v3:
time: 67 us; the launch traced here: 66.7 us
  Pallas kernels  48.9 us (73%)
  starting transfers between devices  12.7 us (19%)
  waiting for transfers between devices  4.1 us (6%)
  local copies, waits for them, and re-layouts  0.71 us (1%)
    pallas_call x2, Pallas kernels, interior(): pl.pallas_call(functools.partial(interior_kernel, (begin, batch, points))...  28.5 us
    all_to_all x2, starting transfers between devices, exchange(): lax.all_to_all(payload, ('chip', 'cores'), split_axis=0, concat_axis=0, t...  12.7 us
    pallas_call x1, Pallas kernels, shards(): pl.pallas_call(functools.partial(pack_kernel, (fields, devices, per_devic...  7.15 us
    pallas_call x1, Pallas kernels, shards(): pl.pallas_call(functools.partial(finish_kernel, (per_device, capacity, wi...  6.32 us
    pallas_call x1, Pallas kernels, shards(): pl.pallas_call(functools.partial(owner_kernel, (devices, capacity, window...  4.65 us
    all_to_all x2, waiting for transfers between devices, exchange(): lax.all_to_all(payload, ('chip', 'cores'), split_axis=0, concat_axis=0, t...  4.1 us
    pallas_call x1, Pallas kernels, shards(): pl.pallas_call(functools.partial(tables_kernel, (fields, devices, per_dev...  2.34 us
  transfers between devices with their start and end apart: 2, of which 2 were waited for; matrix products, arithmetic and copies ran while one was open for 1% of the time, Pallas kernels for 46%

profile of v3, /device:TPU:0, one launch (start us, length us, event | category | flops | bytes accessed | tf_op | source)
XLA Modules:
  0.0 66.7 jit_solution(7647136470723642835)
XLA Ops:
  0.0 0.0 copy-start.2
  0.0 0.0 copy-start.1
  0.0 7.1 %pack.1 = f32[32,40,128]{2,1,0:T(8,128)} custom-call(s32[1]{0:T(128)} %bitcast.me_ref._, s32[1,4096]{1,0:T(1,128)} %bitcast.12, s32[4,4096]{1,0:T(4,128)} %bitcast.9, f32[16,6,128,128]{3,2,1,0:T(8,128)} %field_ref.5), custom_call_target="tpu_custom_call" | custom-call | tf_op jit(solution)/shard_map/pack/pallas_call | solution.py:550
  7.2 7.3 %all-to-all-start = ((f32[32,40,128]{2,1,0:T(8,128)}), f32[32,40,128]{2,1,0:T(8,128)S(1)}, u32[]{:S(2)}, u32[]{:S(2)}) async-start(f32[32,40,128]{2,1,0:T(8,128)} %pack.1), calls=%async_computation | async-start | bytes 1310720 | tf_op jit(solution)/shard_map/all_to_all | solution.py:513
  14.5 0.0 copy-done.2
  14.5 0.6 copy.14
  15.1 0.0 copy-done.1
  15.1 0.1 copy.12.coupling_ref
  15.2 2.3 %tables.1 = (bf16[64,512]{1,0:T(8,128)(2,1)}, s32[256,128]{1,0:T(8,128)}, bf16[128,512]{1,0:T(8,128)(2,1)}, bf16[256,256]{1,0:T(8,128)(2,1)}, s32[128,128]{1,0:T...) custom-call(s32[1]{0:T(128)} %bitcast.me_ref._, ...), custom_call_target="tpu_custom_call" | custom-call | tf_op jit(solution)/shard_map/tables/pallas_call | solution.py:579
  17.5 14.1 %interior.2.first_ref = f32[8,6,128,128]{3,2,1,0:T(8,128)} custom-call(f32[16,180]{1,0:T(8,128)S(1)} %copy.12.coupling_ref, s32[1]{0:T(128)} %bitcast.me_ref._, f32[16,6,128,128]{3,2,1,0:T(8,128)} %field_ref.5, f32[16,6,128,128]{3,2,1,0:T(8,128)} %table_ref.3), custom_call_target="tpu_custom_call" | custom-call | flops 3623878656 | bytes 9437184 | tf_op jit(solution)/shard_map/interior/pallas_call | solution.py:604
  31.7 0.7 %all-to-all-done.arrived_ref = f32[32,40,128]{2,1,0:T(8,128)S(1)} async-done(((f32[32,40,128]{2,1,0:T(8,128)}), f32[32,40,128]{2,1,0:T(8,128)S(1)}, u32[]{:S(2)}, u32[]{:S(2)}) %all-to-all-start) | async-done | bytes 655392 | tf_op jit(solution)/shard_map/all_to_all | solution.py:513
  32.4 4.6 %owner.1 = f32[32,40,128]{2,1,0:T(8,128)} custom-call(f32[32,40,128]{2,1,0:T(8,128)S(1)} %all-to-all-done.arrived_ref, f32[2,64,128]{2,1,0:T(8,128)} %bitcast.11, bf16[128,512]{1,0:T(8,128)(2,1)} %get-tuple-element.21.taker_ref, bf16[256,256]{1,0:T(8,128)(2,1)} %get-tuple-element.22.giver_ref, s32[128,128]{1,0:T(8,128)} %get-tuple-element.23.centre_ref, ...), custom_call_target="tpu_custom_call" | custom-call | tf_op jit(solution)/shard_map/owner/pallas_call | solution.py:626
  37.0 5.4 %all-to-all-start.1 = ((f32[32,40,128]{2,1,0:T(8,128)}), f32[32,40,128]{2,1,0:T(8,128)}, u32[]{:S(2)}, u32[]{:S(2)}) async-start(f32[32,40,128]{2,1,0:T(8,128)} %owner.1), calls=%async_computation.1 | async-start | bytes 1310720 | tf_op jit(solution)/shard_map/all_to_all | solution.py:513
  42.5 0.0 copy-start
  42.5 14.3 %interior.3.second_ref = f32[8,6,128,128]{3,2,1,0:T(8,128)} custom-call(f32[16,180]{1,0:T(8,128)S(1)} %copy.12.coupling_ref, s32[1]{0:T(128)} %bitcast.me_ref._, f32[16,6,128,128]{3,2,1,0:T(8,128)} %field_ref.5, f32[16,6,128,128]{3,2,1,0:T(8,128)} %table_ref.3), custom_call_target="tpu_custom_call" | custom-call | flops 3623878656 | bytes 9437184 | tf_op jit(solution)/shard_map/interior/pallas_call | solution.py:604
  56.8 3.4 %all-to-all-done.1.arrived_ref = f32[32,40,128]{2,1,0:T(8,128)} async-done(((f32[32,40,128]{2,1,0:T(8,128)}), f32[32,40,128]{2,1,0:T(8,128)}, u32[]{:S(2)}, u32[]{:S(2)}) %all-to-all-start.1) | async-done | bytes 655392 | tf_op jit(solution)/shard_map/all_to_all | solution.py:513
  60.2 0.0 copy-done
  60.2 6.3 %finish.1 = f32[16,6,128,128]{3,2,1,0:T(8,128)} custom-call(bf16[64,512]{1,0:T(8,128)(2,1)} %get-tuple-element.29.gather_ref, s32[256,128]{1,0:T(8,128)} %get-tuple-element.30.start_ref, f32[32,40,128]{2,1,0:T(8,128)} %all-to-all-done.1.arrived_ref, f32[8,6,128,128]{3,2,1,0:T(8,128)S(1)} %copy-done, f32[8,6,128,128]{3,2,1,0:T(8,128)} %interior.3.second_ref), custom_call_target="tpu_custom_call" | custom-call | tf_op jit(solution)/shard_map/finish/pallas_call | solution.py:643
  (1 shorter events, 0.0 us)
Async XLA Ops:
  0.0 14.5 %copy-start.2 = (f32[64,2,128]{2,1,0:T(2,128)S(1)}, f32[64,2,128]{2,1,0:T(2,128)}, u32[]{:S(2)}) copy-start(f32[64,2,128]{2,1,0:T(2,128)} %param.12) | copy-start | bytes 196612
  0.0 15.1 %copy-start.1 = (f32[16,5,6,6]{0,3,2,1:T(8,128)S(1)}, f32[16,5,6,6]{0,3,2,1:T(8,128)}, u32[]{:S(2)}) copy-start(f32[16,5,6,6]{0,3,2,1:T(8,128)} %param.9) | copy-start | bytes 34564
  7.2 25.2 %all-to-all-start = ((f32[32,40,128]{2,1,0:T(8,128)}), f32[32,40,128]{2,1,0:T(8,128)S(1)}, u32[]{:S(2)}, u32[]{:S(2)}) async-start(f32[32,40,128]{2,1,0:T(8,128)} %pack.1), calls=%async_computation | async-start | bytes 1310720 | tf_op jit(solution)/shard_map/all_to_all | solution.py:513
  37.0 23.1 %all-to-all-start.1 = ((f32[32,40,128]{2,1,0:T(8,128)}), f32[32,40,128]{2,1,0:T(8,128)}, u32[]{:S(2)}, u32[]{:S(2)}) async-start(f32[32,40,128]{2,1,0:T(8,128)} %owner.1), calls=%async_computation.1 | async-start | bytes 1310720 | tf_op jit(solution)/shard_map/all_to_all | solution.py:513
  42.5 17.7 %copy-start = (f32[8,6,128,128]{3,2,1,0:T(8,128)S(1)}, f32[8,6,128,128]{3,2,1,0:T(8,128)}, u32[]{:S(2)}) copy-start(f32[8,6,128,128]{3,2,1,0:T(8,128)} %interior.2.first_ref) | copy-start | bytes 9437188

commit v4 on v3

--- a/solution.py
+++ b/solution.py
@@ -125,7 +125,17 @@
 
 
 def pack_kernel(
-    cfg, me_ref, device_ref, detail_ref, field_ref, out_ref, held_ref, strips_ref, arrival
+    cfg,
+    me_ref,
+    device_ref,
+    detail_ref,
+    field_ref,
+    out_ref,
+    held_ref,
+    strips_ref,
+    staged_ref,
+    arrival,
+    leaving,
 ):
     fields, owners, per_device, capacity, window, batch, points = cfg
     edges = EDGES * per_device
@@ -143,17 +153,21 @@
     base = iota((slots, points), 1) + start - 1
 
     lane = iota((points, points), 1)
+    lane_of = iota((1, ROWS, points), 2)
     rows = EDGES * batch
     sub = iota((rows, points), 0)
     for step in range(per_device // batch):
-        columns = jnp.zeros((points, points), F32)
+        columns = jnp.zeros((points // ROWS, ROWS, points), F32)
         for b in range(batch):
             patch = step * batch + b
             loads[patch].wait()
             for c in range(6):
                 at = EDGES * (c * batch + b)
                 moved = pltpu.roll(held_ref[patch, c], (2 + at) % points, 1)
-                columns = jnp.where((lane >= at) & (lane < at + EDGES), moved, columns)
+                moved = moved.reshape(columns.shape)
+                hit = jnp.broadcast_to(lane_of // EDGES == at // EDGES, columns.shape)
+                columns = jnp.where(hit, moved, columns)
+        columns = columns.reshape(points, points)
         other = jnp.where(
             lane % EDGES == 1, pltpu.roll(columns, 1, 1), pltpu.roll(columns, points - 1, 1)
         )
@@ -178,12 +192,18 @@
         lane_gather(picked[:, c * points : (c + 1) * points], base & (points - 1))
         for c in range(5)
     ]
-    last = picked[:, 5 * points :]
-    pieces = [
-        lane_gather(last, (base - (window - quarter * at)) & (points - 1)) for at in range(4)
-    ]
+    last = lane_gather(picked[:, 5 * points :], base & (points - 1))
+    pieces = [pltpu.roll(last, window - quarter * at, 1) for at in range(4)]
+    copies = []
     for at, tile in enumerate(fold_window(tiles, pieces, window)):
-        out_ref[:, at * capacity : (at + 1) * capacity, :] = tile.reshape(owners, capacity, points)
+        part = pl.ds(at * capacity, capacity)
+        staged_ref[:, part, :] = tile.reshape(owners, capacity, points)
+        copies.append(
+            pltpu.make_async_copy(staged_ref.at[:, part], out_ref.at[:, part], leaving.at[at])
+        )
+        copies[-1].start()
+    for copy in copies:
+        copy.wait()
 
 
 def read_slots(ref, capacity, window):
@@ -448,14 +468,16 @@
     per_device, capacity, window, batch, points = cfg
     edges = EDGES * per_device
     steps = per_device // batch
-    half = steps // 2
+    half = first_ref.shape[0]
     loads, stores = [], []
     for step in range(steps):
-        source = first_ref if step < half else second_ref
-        block = pl.ds(step % half * batch, batch)
         own = held_ref.at[pl.ds(step * batch, batch)]
-        loads.append(pltpu.make_async_copy(source.at[block], own, arrival.at[step]))
-        loads[-1].start()
+        if step * batch >= half:
+            block = pl.ds(step * batch - half, batch)
+            loads.append(pltpu.make_async_copy(second_ref.at[block], own, arrival.at[step]))
+            loads[-1].start()
+        else:
+            loads.append(None)
         stores.append(
             pltpu.make_async_copy(own, out_ref.at[pl.ds(step * batch, batch)], leaving.at[step])
         )
@@ -489,11 +511,14 @@
     for step in range(steps):
         select = jnp.where(ahead == step * batch, weight, 0.0).astype(BF16)
         add = dot(turned_ref[...], select)
-        loads[step].wait()
+        inner_ref = first_ref
+        if loads[step] is not None:
+            loads[step].wait()
+            inner_ref = held_ref
         for b in range(batch):
             patch = step * batch + b
             for c in range(6):
-                value = held_ref[patch, c]
+                value = inner_ref[patch, c]
                 value = value + add[c * points : (c + 1) * points, b * points : (b + 1) * points]
                 top = edge_ref[c, EDGES * patch : EDGES * patch + 1, :]
                 bottom = edge_ref[c, EDGES * patch + 3 : EDGES * patch + 4, :]
@@ -560,11 +585,13 @@
             whole(detail_rows.shape),
             pl.BlockSpec(memory_space=pl.ANY),
         ],
-        out_specs=whole(payload_shape),
+        out_specs=pl.BlockSpec(memory_space=pl.ANY),
         scratch_shapes=[
             pltpu.VMEM(patch_field.shape, F32),
             pltpu.VMEM((6, edges, points), F32),
+            pltpu.VMEM(payload_shape, F32),
             pltpu.SemaphoreType.DMA((per_device,)),
+            pltpu.SemaphoreType.DMA((5,)),
         ],
         compiler_params=params(56),
     )(me, device_row, detail_rows, patch_field)
@@ -638,7 +665,6 @@
     second = in_hbm(interior(half, per_device, back))
     gather = tied(gather, second)
 
-    batch = 2
     anywhere = pl.BlockSpec(memory_space=pl.ANY)
     return pl.pallas_call(
         functools.partial(finish_kernel, (per_device, capacity, window, batch, points)),
@@ -649,7 +675,7 @@
             whole(gather.shape),
             whole(start_table.shape),
             vmem,
-            anywhere,
+            vmem,
             anywhere,
         ],
         out_specs=anywhere,

time: 67 us -> 65.8 us (0.982)
  Pallas kernels: 48.9 us -> 47.7 us
    pallas_call x1, Pallas kernels: 6.32 us -> 5.14 us  [shards(): pl.pallas_call(functools.partial(finish_kernel, (per_device, capacity, wi...]
  transfers between devices with their start and end apart: 2 -> 2, of which waited for: 2 -> 2; matrix products, arithmetic and copies ran while one was open for 1% -> 1% of each run, Pallas kernels for 46% -> 47%
where the time goes in v4:
time: 65.8 us; the launch traced here: 65.4 us
  Pallas kernels  47.7 us (72%)
  starting transfers between devices  12.7 us (19%)
  waiting for transfers between devices  4.09 us (6%)
  local copies, waits for them, and re-layouts  0.71 us (1%)
    pallas_call x2, Pallas kernels, interior(): pl.pallas_call(functools.partial(interior_kernel, (begin, batch, points))...  28.5 us
    all_to_all x2, starting transfers between devices, exchange(): lax.all_to_all(payload, ('chip', 'cores'), split_axis=0, concat_axis=0, t...  12.7 us
    pallas_call x1, Pallas kernels, shards(): pl.pallas_call(functools.partial(pack_kernel, (fields, devices, per_devic...  7.04 us
    pallas_call x1, Pallas kernels, shards(): pl.pallas_call(functools.partial(finish_kernel, (per_device, capacity, wi...  5.14 us
    pallas_call x1, Pallas kernels, shards(): pl.pallas_call(functools.partial(owner_kernel, (devices, capacity, window...  4.65 us
    all_to_all x2, waiting for transfers between devices, exchange(): lax.all_to_all(payload, ('chip', 'cores'), split_axis=0, concat_axis=0, t...  4.09 us
    pallas_call x1, Pallas kernels, shards(): pl.pallas_call(functools.partial(tables_kernel, (fields, devices, per_dev...  2.34 us
  transfers between devices with their start and end apart: 2, of which 2 were waited for; matrix products, arithmetic and copies ran while one was open for 1% of the time, Pallas kernels for 47%

profile of v4, /device:TPU:0, one launch (start us, length us, event | category | flops | bytes accessed | tf_op | source)
XLA Modules:
  0.0 65.4 jit_solution(3437866685742746571)
XLA Ops:
  0.0 0.0 copy-start.2
  0.0 0.0 copy-start.1
  0.0 7.0 %pack.1 = f32[32,40,128]{2,1,0:T(8,128)} custom-call(s32[1]{0:T(128)} %bitcast.me_ref._, s32[1,4096]{1,0:T(1,128)} %bitcast.12, s32[4,4096]{1,0:T(4,128)} %bitcast.9, f32[16,6,128,128]{3,2,1,0:T(8,128)} %field_ref.5), custom_call_target="tpu_custom_call" | custom-call | tf_op jit(solution)/shard_map/pack/pallas_call | solution.py:575
  7.1 7.3 %all-to-all-start = ((f32[32,40,128]{2,1,0:T(8,128)}), f32[32,40,128]{2,1,0:T(8,128)S(1)}, u32[]{:S(2)}, u32[]{:S(2)}) async-start(f32[32,40,128]{2,1,0:T(8,128)} %pack.1), calls=%async_computation | async-start | bytes 1310720 | tf_op jit(solution)/shard_map/all_to_all | solution.py:538
  14.4 0.0 copy-done.2
  14.4 0.6 copy.14
  15.0 0.0 copy-done.1
  15.0 0.1 copy.12.coupling_ref
  15.1 2.3 %tables.1 = (bf16[64,512]{1,0:T(8,128)(2,1)}, s32[256,128]{1,0:T(8,128)}, bf16[128,512]{1,0:T(8,128)(2,1)}, bf16[256,256]{1,0:T(8,128)(2,1)}, s32[128,128]{1,0:T...) custom-call(s32[1]{0:T(128)} %bitcast.me_ref._, ...), custom_call_target="tpu_custom_call" | custom-call | tf_op jit(solution)/shard_map/tables/pallas_call | solution.py:606
  17.4 14.1 %interior.2.first_ref = f32[8,6,128,128]{3,2,1,0:T(8,128)} custom-call(f32[16,180]{1,0:T(8,128)S(1)} %copy.12.coupling_ref, s32[1]{0:T(128)} %bitcast.me_ref._, f32[16,6,128,128]{3,2,1,0:T(8,128)} %field_ref.5, f32[16,6,128,128]{3,2,1,0:T(8,128)} %table_ref.3), custom_call_target="tpu_custom_call" | custom-call | flops 3623878656 | bytes 9437184 | tf_op jit(solution)/shard_map/interior/pallas_call | solution.py:631
  31.6 0.7 %all-to-all-done.arrived_ref = f32[32,40,128]{2,1,0:T(8,128)S(1)} async-done(((f32[32,40,128]{2,1,0:T(8,128)}), f32[32,40,128]{2,1,0:T(8,128)S(1)}, u32[]{:S(2)}, u32[]{:S(2)}) %all-to-all-start) | async-done | bytes 655392 | tf_op jit(solution)/shard_map/all_to_all | solution.py:538
  32.3 4.6 %owner.1 = f32[32,40,128]{2,1,0:T(8,128)} custom-call(f32[32,40,128]{2,1,0:T(8,128)S(1)} %all-to-all-done.arrived_ref, f32[2,64,128]{2,1,0:T(8,128)} %bitcast.11, bf16[128,512]{1,0:T(8,128)(2,1)} %get-tuple-element.21.taker_ref, bf16[256,256]{1,0:T(8,128)(2,1)} %get-tuple-element.22.giver_ref, s32[128,128]{1,0:T(8,128)} %get-tuple-element.23.centre_ref, ...), custom_call_target="tpu_custom_call" | custom-call | tf_op jit(solution)/shard_map/owner/pallas_call | solution.py:653
  36.9 5.4 %all-to-all-start.1 = ((f32[32,40,128]{2,1,0:T(8,128)}), f32[32,40,128]{2,1,0:T(8,128)}, u32[]{:S(2)}, u32[]{:S(2)}) async-start(f32[32,40,128]{2,1,0:T(8,128)} %owner.1), calls=%async_computation.1 | async-start | bytes 1310720 | tf_op jit(solution)/shard_map/all_to_all | solution.py:538
  42.4 0.0 copy-start
  42.4 14.3 %interior.3.second_ref = f32[8,6,128,128]{3,2,1,0:T(8,128)} custom-call(f32[16,180]{1,0:T(8,128)S(1)} %copy.12.coupling_ref, s32[1]{0:T(128)} %bitcast.me_ref._, f32[16,6,128,128]{3,2,1,0:T(8,128)} %field_ref.5, f32[16,6,128,128]{3,2,1,0:T(8,128)} %table_ref.3), custom_call_target="tpu_custom_call" | custom-call | flops 3623878656 | bytes 9437184 | tf_op jit(solution)/shard_map/interior/pallas_call | solution.py:631
  56.7 3.4 %all-to-all-done.1.arrived_ref = f32[32,40,128]{2,1,0:T(8,128)} async-done(((f32[32,40,128]{2,1,0:T(8,128)}), f32[32,40,128]{2,1,0:T(8,128)}, u32[]{:S(2)}, u32[]{:S(2)}) %all-to-all-start.1) | async-done | bytes 655392 | tf_op jit(solution)/shard_map/all_to_all | solution.py:538
  60.1 0.0 copy-done
  60.1 5.1 %finish.1 = f32[16,6,128,128]{3,2,1,0:T(8,128)} custom-call(bf16[64,512]{1,0:T(8,128)(2,1)} %get-tuple-element.29.gather_ref, s32[256,128]{1,0:T(8,128)} %get-tuple-element.30.start_ref, f32[32,40,128]{2,1,0:T(8,128)} %all-to-all-done.1.arrived_ref, f32[8,6,128,128]{3,2,1,0:T(8,128)S(1)} %copy-done, f32[8,6,128,128]{3,2,1,0:T(8,128)} %interior.3.second_ref), custom_call_target="tpu_custom_call" | custom-call | tf_op jit(solution)/shard_map/finish/pallas_call | solution.py:669
  (1 shorter events, 0.0 us)
Async XLA Ops:
  0.0 14.4 %copy-start.2 = (f32[64,2,128]{2,1,0:T(2,128)S(1)}, f32[64,2,128]{2,1,0:T(2,128)}, u32[]{:S(2)}) copy-start(f32[64,2,128]{2,1,0:T(2,128)} %param.12) | copy-start | bytes 196612
  0.0 15.0 %copy-start.1 = (f32[16,5,6,6]{0,3,2,1:T(8,128)S(1)}, f32[16,5,6,6]{0,3,2,1:T(8,128)}, u32[]{:S(2)}) copy-start(f32[16,5,6,6]{0,3,2,1:T(8,128)} %param.9) | copy-start | bytes 34564
  7.1 25.2 %all-to-all-start = ((f32[32,40,128]{2,1,0:T(8,128)}), f32[32,40,128]{2,1,0:T(8,128)S(1)}, u32[]{:S(2)}, u32[]{:S(2)}) async-start(f32[32,40,128]{2,1,0:T(8,128)} %pack.1), calls=%async_computation | async-start | bytes 1310720 | tf_op jit(solution)/shard_map/all_to_all | solution.py:538
  36.9 23.2 %all-to-all-start.1 = ((f32[32,40,128]{2,1,0:T(8,128)}), f32[32,40,128]{2,1,0:T(8,128)}, u32[]{:S(2)}, u32[]{:S(2)}) async-start(f32[32,40,128]{2,1,0:T(8,128)} %owner.1), calls=%async_computation.1 | async-start | bytes 1310720 | tf_op jit(solution)/shard_map/all_to_all | solution.py:538
  42.4 17.7 %copy-start = (f32[8,6,128,128]{3,2,1,0:T(8,128)S(1)}, f32[8,6,128,128]{3,2,1,0:T(8,128)}, u32[]{:S(2)}) copy-start(f32[8,6,128,128]{3,2,1,0:T(8,128)} %interior.2.first_ref) | copy-start | bytes 9437188

commit v5 on v4

--- a/solution.py
+++ b/solution.py
@@ -216,14 +216,24 @@
     return tiles
 
 
+def slots_kernel(cfg, me_ref, device_ref, detail_ref, gather_ref, start_ref):
+    fields, owners, per_device, capacity, points = cfg
+    edges = EDGES * per_device
+    slots = owners * capacity
+    code = side_codes(fields, device_ref[...], detail_ref)
+    row, start = slot_tables(fields, code, me_ref[0], owners, capacity)
+    picker = jnp.where(iota((slots, 2 * edges), 1) % edges == row, 1.0, 0.0)
+    gather = jnp.transpose(picker)[:edges].astype(BF16)
+    gather_ref[...] = jnp.concatenate([gather, gather], axis=1)
+    start_ref[...] = jnp.broadcast_to(start, (slots, points))
+
+
 def tables_kernel(
     cfg,
     me_ref,
     device_ref,
     detail_ref,
     angle_ref,
-    gather_ref,
-    start_ref,
     taker_ref,
     giver_ref,
     centre_ref,
@@ -233,18 +243,10 @@
     frame_ref,
 ):
     fields, owners, per_device, capacity, points = cfg
-    edges = EDGES * per_device
     slots = owners * capacity
     sides = device_ref.shape[1] // owners
     owned = sides // 2
     me = me_ref[0]
-    code = side_codes(fields, device_ref[...], detail_ref)
-    row, start = slot_tables(fields, code, me, owners, capacity)
-    picker = jnp.where(iota((slots, 2 * edges), 1) % edges == row, 1.0, 0.0)
-    gather = jnp.transpose(picker)[:edges].astype(BF16)
-    gather_ref[...] = jnp.concatenate([gather, gather], axis=1)
-    start_ref[...] = jnp.broadcast_to(start, (slots, points))
-
     own = pl.ds(pl.multiple_of(me * sides, sides), sides)
     own_code = fields.pack(device_ref[:, own], [detail_ref[i : i + 1, own] for i in range(4)])
     code_row = jnp.broadcast_to(own_code, (sides, sides))
@@ -607,8 +609,6 @@
         functools.partial(tables_kernel, (fields, devices, per_device, capacity, points)),
         name="tables",
         out_shape=[
-            table((edges, 2 * slots), BF16),
-            table((slots, points), I32),
             table((sides, 2 * slots), BF16),
             table((slots, 2 * sides), BF16),
             table((sides, points), I32),
@@ -618,11 +618,10 @@
             table((9, owned, points), F32),
         ],
         in_specs=[smem] + [vmem] * 3,
-        out_specs=[vmem] * 9,
+        out_specs=[vmem] * 7,
         compiler_params=params(56),
     )(tied(me, outgoing), device_row, detail_rows, angles.T)
     tables = [in_hbm(value) for value in tables]
-    gather, start_table = tables[:2]
 
     def interior(begin, end, after):
         count = end - begin
@@ -648,7 +647,7 @@
     half = per_device // 2
     first = interior(0, half, outgoing)
     weights = tied(weights, first)
-    taker, giver, centre, near, opening, spread, frame = tables[2:]
+    taker, giver, centre, near, opening, spread, frame = tables
     held = (taker, centre, near, weights, frame, opening, spread, giver)
     back = pl.pallas_call(
         functools.partial(owner_kernel, (devices, capacity, window, points)),
@@ -660,10 +659,19 @@
         + [pltpu.VMEM(t.shape, t.dtype) for t in held]
         + [pltpu.SemaphoreType.DMA((len(held),))],
         compiler_params=params(40),
-    )(arrived, weights, *tables[2:])
+    )(arrived, weights, *tables)
     returned = exchange(back)
     second = in_hbm(interior(half, per_device, back))
-    gather = tied(gather, second)
+    gather, start_table = pl.pallas_call(
+        functools.partial(slots_kernel, (fields, devices, per_device, capacity, points)),
+        name="slots",
+        out_shape=[table((edges, 2 * slots), BF16), table((slots, points), I32)],
+        in_specs=[smem] + [vmem] * 2,
+        out_specs=[vmem] * 2,
+        compiler_params=params(56),
+    )(tied(me, back), device_row, detail_rows)
+    gather = in_hbm(tied(gather, second))
+    start_table = in_hbm(start_table)
 
     anywhere = pl.BlockSpec(memory_space=pl.ANY)
     return pl.pallas_call(

time: 65.8 us -> 65.7 us (level)
  waiting for transfers between devices: 4.09 us -> 2.47 us
  Pallas kernels: 47.7 us -> 49.3 us
    pallas_call x0 -> x1, Pallas kernels: none -> 1.82 us  [shards(): pl.pallas_call(functools.partial(slots_kernel, (fields, devices, per_devi...]
    all_to_all x2, waiting for transfers between devices: 4.09 us -> 2.47 us  [exchange(): lax.all_to_all(payload, ('chip', 'cores'), split_axis=0, concat_axis=0, t...]
  transfers between devices with their start and end apart: 2 -> 2, of which waited for: 2 -> 2; matrix products, arithmetic and copies ran while one was open for 1% -> 1% of each run, Pallas kernels for 47% -> 50%
where the time goes in v5:
time: 65.7 us; the launch traced here: 65.3 us
  Pallas kernels  49.3 us (75%)
  starting transfers between devices  12.6 us (19%)
  waiting for transfers between devices  2.47 us (4%)
  local copies, waits for them, and re-layouts  0.72 us (1%)
    pallas_call x2, Pallas kernels, interior(): pl.pallas_call(functools.partial(interior_kernel, (begin, batch, points))...  28.5 us
    all_to_all x2, starting transfers between devices, exchange(): lax.all_to_all(payload, ('chip', 'cores'), split_axis=0, concat_axis=0, t...  12.6 us
    pallas_call x1, Pallas kernels, shards(): pl.pallas_call(functools.partial(pack_kernel, (fields, devices, per_devic...  7.06 us
    pallas_call x1, Pallas kernels, shards(): pl.pallas_call(functools.partial(finish_kernel, (per_device, capacity, wi...  5.14 us
    pallas_call x1, Pallas kernels, shards(): pl.pallas_call(functools.partial(owner_kernel, (devices, capacity, window...  4.64 us
    all_to_all x2, waiting for transfers between devices, exchange(): lax.all_to_all(payload, ('chip', 'cores'), split_axis=0, concat_axis=0, t...  2.47 us
    pallas_call x1, Pallas kernels, shards(): pl.pallas_call(functools.partial(tables_kernel, (fields, devices, per_dev...  2.16 us
    pallas_call x1, Pallas kernels, shards(): pl.pallas_call(functools.partial(slots_kernel, (fields, devices, per_devi...  1.82 us
  transfers between devices with their start and end apart: 2, of which 2 were waited for; matrix products, arithmetic and copies ran while one was open for 1% of the time, Pallas kernels for 50%

profile of v5, /device:TPU:0, one launch (start us, length us, event | category | flops | bytes accessed | tf_op | source)
XLA Modules:
  0.0 65.3 jit_solution(1468418454720854028)
XLA Ops:
  0.0 0.0 copy-start.2
  0.0 0.0 copy-start.1
  0.0 7.1 %pack.1 = f32[32,40,128]{2,1,0:T(8,128)} custom-call(s32[1]{0:T(128)} %bitcast.me_ref._, s32[1,4096]{1,0:T(1,128)} %bitcast.13, s32[4,4096]{1,0:T(4,128)} %bitcast.9, f32[16,6,128,128]{3,2,1,0:T(8,128)} %field_ref.5), custom_call_target="tpu_custom_call" | custom-call | tf_op jit(solution)/shard_map/pack/pallas_call | solution.py:577
  7.1 7.3 %all-to-all-start = ((f32[32,40,128]{2,1,0:T(8,128)}), f32[32,40,128]{2,1,0:T(8,128)S(1)}, u32[]{:S(2)}, u32[]{:S(2)}) async-start(f32[32,40,128]{2,1,0:T(8,128)} %pack.1), calls=%async_computation | async-start | bytes 1310720 | tf_op jit(solution)/shard_map/all_to_all | solution.py:540
  14.4 0.0 copy-done.2
  14.4 0.6 copy.14
  15.0 0.0 copy-done.1
  15.1 0.1 copy.11.coupling_ref
  15.1 2.2 %tables.1 = (bf16[128,512]{1,0:T(8,128)(2,1)}, bf16[256,256]{1,0:T(8,128)(2,1)}, s32[128,128]{1,0:T(8,128)}, f32[3,128,128]{2,1,0:T(8,128)}, s32[128,128]{1,0:T(...) custom-call(s32[1]{0:T(128)} %bitcast.me_ref._, s32[1,4096]{1,0:T(1,128)} %bitcast.14, s32[4,4096]{1,0:T(4,128)} %bitcast.10, ...), custom_call_target="tpu_custom_call" | custom-call | tf_op jit(solution)/shard_map/tables/pallas_call | solution.py:608
  17.3 14.1 %interior.2.first_ref = f32[8,6,128,128]{3,2,1,0:T(8,128)} custom-call(f32[16,180]{1,0:T(8,128)S(1)} %copy.11.coupling_ref, s32[1]{0:T(128)} %bitcast.me_ref._, f32[16,6,128,128]{3,2,1,0:T(8,128)} %field_ref.5, f32[16,6,128,128]{3,2,1,0:T(8,128)} %table_ref.3), custom_call_target="tpu_custom_call" | custom-call | flops 3623878656 | bytes 9437184 | tf_op jit(solution)/shard_map/interior/pallas_call | solution.py:630
  31.4 0.9 %all-to-all-done.arrived_ref = f32[32,40,128]{2,1,0:T(8,128)S(1)} async-done(((f32[32,40,128]{2,1,0:T(8,128)}), f32[32,40,128]{2,1,0:T(8,128)S(1)}, u32[]{:S(2)}, u32[]{:S(2)}) %all-to-all-start) | async-done | bytes 655392 | tf_op jit(solution)/shard_map/all_to_all | solution.py:540
  32.3 4.6 %owner.1 = f32[32,40,128]{2,1,0:T(8,128)} custom-call(f32[32,40,128]{2,1,0:T(8,128)S(1)} %all-to-all-done.arrived_ref, f32[2,64,128]{2,1,0:T(8,128)} %bitcast.12, bf16[128,512]{1,0:T(8,128)(2,1)} %get-tuple-element.20.taker_ref, bf16[256,256]{1,0:T(8,128)(2,1)} %get-tuple-element.21.giver_ref, s32[128,128]{1,0:T(8,128)} %get-tuple-element.22.centre_ref, ...), custom_call_target="tpu_custom_call" | custom-call | tf_op jit(solution)/shard_map/owner/pallas_call | solution.py:652
  37.0 5.3 %all-to-all-start.1 = ((f32[32,40,128]{2,1,0:T(8,128)}), f32[32,40,128]{2,1,0:T(8,128)}, u32[]{:S(2)}, u32[]{:S(2)}) async-start(f32[32,40,128]{2,1,0:T(8,128)} %owner.1), calls=%async_computation.1 | async-start | bytes 1310720 | tf_op jit(solution)/shard_map/all_to_all | solution.py:540
  42.2 1.8 %slots.1 = (bf16[64,512]{1,0:T(8,128)(2,1)}, s32[256,128]{1,0:T(8,128)}) custom-call(s32[1]{0:T(128)} %bitcast.me_ref._, s32[1,4096]{1,0:T(1,128)} %bitcast.15, s32[4,4096]{1,0:T(4,128)} %bitcast.11), custom_call_target="tpu_custom_call" | custom-call | tf_op jit(solution)/shard_map/slots/pallas_call | solution.py:665
  44.0 0.0 copy-start
  44.0 14.3 %interior.3.second_ref = f32[8,6,128,128]{3,2,1,0:T(8,128)} custom-call(f32[16,180]{1,0:T(8,128)S(1)} %copy.11.coupling_ref, s32[1]{0:T(128)} %bitcast.me_ref._, f32[16,6,128,128]{3,2,1,0:T(8,128)} %field_ref.5, f32[16,6,128,128]{3,2,1,0:T(8,128)} %table_ref.3), custom_call_target="tpu_custom_call" | custom-call | flops 3623878656 | bytes 9437184 | tf_op jit(solution)/shard_map/interior/pallas_call | solution.py:630
  58.4 1.6 %all-to-all-done.1.arrived_ref = f32[32,40,128]{2,1,0:T(8,128)} async-done(((f32[32,40,128]{2,1,0:T(8,128)}), f32[32,40,128]{2,1,0:T(8,128)}, u32[]{:S(2)}, u32[]{:S(2)}) %all-to-all-start.1) | async-done | bytes 655392 | tf_op jit(solution)/shard_map/all_to_all | solution.py:540
  59.9 0.0 copy-done
  59.9 5.1 %finish.1 = f32[16,6,128,128]{3,2,1,0:T(8,128)} custom-call(bf16[64,512]{1,0:T(8,128)(2,1)} %get-tuple-element.29.gather_ref, s32[256,128]{1,0:T(8,128)} %get-tuple-element.30.start_ref, f32[32,40,128]{2,1,0:T(8,128)} %all-to-all-done.1.arrived_ref, f32[8,6,128,128]{3,2,1,0:T(8,128)S(1)} %copy-done, f32[8,6,128,128]{3,2,1,0:T(8,128)} %interior.3.second_ref), custom_call_target="tpu_custom_call" | custom-call | tf_op jit(solution)/shard_map/finish/pallas_call | solution.py:677
  (1 shorter events, 0.0 us)
Async XLA Ops:
  0.0 14.4 %copy-start.2 = (f32[64,2,128]{2,1,0:T(2,128)S(1)}, f32[64,2,128]{2,1,0:T(2,128)}, u32[]{:S(2)}) copy-start(f32[64,2,128]{2,1,0:T(2,128)} %param.12) | copy-start | bytes 196612
  0.0 15.0 %copy-start.1 = (f32[16,5,6,6]{0,3,2,1:T(8,128)S(1)}, f32[16,5,6,6]{0,3,2,1:T(8,128)}, u32[]{:S(2)}) copy-start(f32[16,5,6,6]{0,3,2,1:T(8,128)} %param.9) | copy-start | bytes 34564
  7.1 25.2 %all-to-all-start = ((f32[32,40,128]{2,1,0:T(8,128)}), f32[32,40,128]{2,1,0:T(8,128)S(1)}, u32[]{:S(2)}, u32[]{:S(2)}) async-start(f32[32,40,128]{2,1,0:T(8,128)} %pack.1), calls=%async_computation | async-start | bytes 1310720 | tf_op jit(solution)/shard_map/all_to_all | solution.py:540
  37.0 23.0 %all-to-all-start.1 = ((f32[32,40,128]{2,1,0:T(8,128)}), f32[32,40,128]{2,1,0:T(8,128)}, u32[]{:S(2)}, u32[]{:S(2)}) async-start(f32[32,40,128]{2,1,0:T(8,128)} %owner.1), calls=%async_computation.1 | async-start | bytes 1310720 | tf_op jit(solution)/shard_map/all_to_all | solution.py:540
  44.0 15.9 %copy-start = (f32[8,6,128,128]{3,2,1,0:T(8,128)S(1)}, f32[8,6,128,128]{3,2,1,0:T(8,128)}, u32[]{:S(2)}) copy-start(f32[8,6,128,128]{3,2,1,0:T(8,128)} %interior.2.first_ref) | copy-start | bytes 9437188
